TPU v7x, 128 devices: a whole 4x4x4 slice. The times are simulated.
128 devices in a mesh: section: 2 (over z_hi), fsdp: 64 (over y, x, z_lo, core).
Axes of the slice: x: 4, y: 4, z: 4 (z_hi: 2, z_lo: 2; z = z_hi * 2 + z_lo), core: 2. Of those that a mesh axis runs over, the one named last changes fastest.
Arguments:
- tokens_in: bfloat16 [2, 6144, 1024], P(None, 'fsdp'), may hold values from -6 to 6
- attn_proj: bfloat16 [2, 1024, 3072], P('section', 'fsdp'), may hold values from -0.1875 to 0.1875
- attn_out: bfloat16 [2, 1024, 1024], P('section', 'fsdp'), may hold values from -1 to 1
- mlp_in: bfloat16 [2, 1024, 5248], P('section', 'fsdp'), may hold values from -0.1875 to 0.1875
- mlp_out: bfloat16 [2, 1024, 2624], P('section', 'fsdp'), may hold values from -0.125 to 0.125
- gain_attn: bfloat16 [2, 1024], P('section', 'fsdp'), may hold values from 0.25 to 1.75
- gain_mlp: bfloat16 [2, 1024], P('section', 'fsdp'), may hold values from 0.25 to 1.75
- lengths: int32 [2, 64, 4], P(None, 'fsdp'), may hold values from 1 to 78, 96 in all within a row
- cotangent: bfloat16 [2, 6144, 1024], P(None, 'fsdp'), may hold values from -16 to 16
Outputs:
- section_outputs: bfloat16 [2, 2, 6144, 1024], P('section', None, 'fsdp')
- section_input_grads: bfloat16 [2, 2, 6144, 1024], P('section', None, 'fsdp')
- grad_attn_proj: float32 [2, 1024, 3072], P('section', 'fsdp')
- grad_attn_out: float32 [2, 1024, 1024], P('section', 'fsdp')
- grad_mlp_in: float32 [2, 1024, 5248], P('section', 'fsdp')
- grad_mlp_out: float32 [2, 1024, 2624], P('section', 'fsdp')
- grad_gain_attn: float32 [2, 1024], P('section', 'fsdp')
- grad_gain_mlp: float32 [2, 1024], P('section', 'fsdp')
Inputs may be any that keep to these rules, and one draw needn't show every extreme that they name: Each row of 4 lengths sums to 96, and every row's longest is at most 78.
All inputs are finite; a program needn't handle non-finite values.
Results may differ from a plain program's by a relative error of at most 0.025.
Values may be sent and summed in bfloat16 or wider, within the bound.
No kernel may reach another device: no remote copies, remote signals or barrier semaphores. Data moves between devices by JAX's collectives and lax.ppermute only.
A program may use at most 256 MiB of HBM per device.

v0:
```python
import functools
import math
import jax
import jax.numpy as jnp
from jax import lax
from jax.experimental import pallas as pl
from jax.experimental.pallas import tpu as pltpu
from jax.sharding import PartitionSpec as P

HEADS = 16
HEAD_DIM = 64
WINDOW = 128
EPS = 1e-05
NY, NX, NZ, NC = 4, 4, 2, 2
SHARDS = NY * NX * NZ * NC
BF = jnp.bfloat16
F32 = jnp.float32
ATTN_TILE = 1024
MLP_TILE = 896
GAIN_TILE = 128
GROUP = 8
SCALE = HEAD_DIM**-0.5
PARAMS = pltpu.CompilerParams(vmem_limit_bytes=56 * 1024 * 1024)


def split_index(i):
    return i // (NX * NZ * NC), (i // (NZ * NC)) % NX, (i // NC) % NZ, i % NC


def join_index(y, x, z, c):
    return ((y * NX + x) * NZ + z) * NC + c


def pairs(kind, step=1):
    out = []
    for i in range(SHARDS):
        y, x, z, c = split_index(i)
        if kind == "core":
            c = 1 - c
        elif kind == "z":
            z = 1 - z
        elif (kind == "first") == (c == 0):
            y = (y + step) % NY
        else:
            x = (x + step) % NX
        out.append((i, join_index(y, x, z, c)))
    return out


def send(value, kind, step=1):
    return lax.ppermute(value, "fsdp", pairs(kind, step))


def tie(*values):
    return lax.optimization_barrier(values)


def rows(*blocks):
    return jnp.concatenate(blocks, 0)


def spread(block):
    return rows(block, send(block, "second", -1), send(block, "second", 2), send(block, "second", 1))


def near(block):
    return send(block, "first", -1), send(block, "first", 1)


def far(after, before):
    half = after.shape[0] // 2
    return send(after[:half], "first", -1), send(before[half:], "first", 1)


def core(*pieces):
    return tuple(send(piece, "core") for piece in pieces)


def gather(a, m):
    a_z, m = tie(send(a, "z"), m)
    a, m_z = tie(spread(rows(a, a_z)), send(m, "z"))
    a_after, a_before = near(a)
    m = spread(rows(m, m_z))
    a_far, a_far2 = far(a_after, a_before)
    a_far, a_far2, m = tie(a_far, a_far2, m)
    a = (a, a_after, a_far, a_far2, a_before)
    return a + core(*a), (m, *near(m))


def add(left, right):
    return left.astype(F32) + right.astype(F32)


def cut(size):
    quarter = size // 4
    return quarter, quarter, quarter // 2, quarter // 2, quarter


def split(block, sizes):
    edges = [sum(sizes[:k]) for k in range(len(sizes) + 1)]
    return tuple(block[low:high] for low, high in zip(edges[:-1], edges[1:]))


def ring_start(parts, got):
    return tuple(add(part, other) for part, other in zip(parts, split(got, cut(got.shape[0]))))


def ring_mix(after, before, got_a, got_b):
    half = got_a.shape[0]
    after = rows(after[:half] + got_a.astype(F32), after[half:])
    before = rows(before[:half], before[half:] + got_b.astype(F32))
    return after.astype(BF), before.astype(BF)


def ring_close(here, got_c, got_d):
    return (here + got_c.astype(F32) + got_d.astype(F32)).astype(BF)


def direct(block):
    size = block.shape[0] // 4
    here, after, far, before = (block[k * size : (k + 1) * size] for k in range(4))
    return here, send(after, "second", 1), send(far, "second", 2), send(before, "second", -1)


def close_z(here, *got):
    block = (add(here, got[0]) + add(got[1], got[2])).astype(BF)
    mine = block.shape[0] // 2
    return add(block[:mine], send(block[mine:], "z"))


def relative_order(me):
    y, x, z, c = split_index(me)
    place = jnp.arange(SHARDS * 16, dtype=jnp.int32)
    block, inside = place // 16, place % 16
    core_at = c ^ (block // 32)
    first, second = (block // 8) % 4, (block // 2) % 4
    row_y = (y + jnp.where(core_at == 0, first, second)) % NY
    row_x = (x + jnp.where(core_at == 0, second, first)) % NX
    absolute = join_index(row_y, row_x, z ^ (block % 2), core_at) * 16 + inside
    return (place[:, None] == absolute[None, :]).astype(BF)


def dot(left, right):
    return jnp.dot(left, right, preferred_element_type=F32)


def contract_last(left, right):
    return lax.dot_general(left, right, (((1,), (1,)), ((), ())), preferred_element_type=F32)


def contract_first(left, right):
    return lax.dot_general(left, right, (((0,), (0,)), ((), ())), preferred_element_type=F32)


def normal(values):
    centre = jnp.mean(values, -1, keepdims=True)
    centred = values - centre
    scale = lax.rsqrt(jnp.mean(centred * centred, -1, keepdims=True) + EPS)
    return centred * scale, scale


def normal_back(grad, unit, scale):
    return scale * (
        grad
        - jnp.mean(grad, -1, keepdims=True)
        - unit * jnp.mean(grad * unit, -1, keepdims=True)
    )


def segment_info(lens, count):
    ends = jnp.cumsum(lens, axis=-1)
    starts = ends - lens
    places = jnp.arange(count, dtype=jnp.int32)
    segment = jnp.sum((places[:, None] >= ends[..., None, :]).astype(jnp.int32), axis=-1)
    picked = (segment[..., None] == jnp.arange(lens.shape[-1], dtype=jnp.int32)).astype(jnp.int32)
    inner = places - jnp.sum(picked * starts[..., None, :], axis=-1)
    return segment, inner


def to_absolute(values, order):
    high = values.astype(BF)
    low = (values - high.astype(F32)).astype(BF)
    return contract_last(high, order) + contract_last(low, order)


def stack_rows(refs):
    return jnp.concatenate([ref[...] for ref in refs], 0)


def gain_rows(refs):
    row = lax.broadcasted_iota(jnp.int32, (16, 128), 0)
    lane = lax.broadcasted_iota(jnp.int32, (16, 128), 1)
    return contract_last((row == lane).astype(BF), stack_rows(refs))


def partner(values):
    width = values.shape[1]
    lane = lax.broadcasted_iota(jnp.int32, values.shape, 1)
    ahead = pltpu.roll(values, width - HEAD_DIM // 2, 1)
    behind = pltpu.roll(values, HEAD_DIM // 2, 1)
    return jnp.where(lane % HEAD_DIM < HEAD_DIM // 2, -ahead, behind)


def widen(table, width):
    return jnp.concatenate([table] * (width // table.shape[1]), 1)


def pair_bias(col, row):
    same = col[:, 0:1] == row[0:1]
    near = jnp.abs(col[:, 1:2] - row[1:2]) <= col[:, 2:3]
    return jnp.where(same & near, 0.0, -1e30)


def head_of(qkv, part, head, rows):
    return qkv[part, rows, head * HEAD_DIM : (head + 1) * HEAD_DIM]


def attn_forward_kernel(n, micro, steps, *refs):
    u, order, cos, sin, col, row = refs[:6]
    proj, out, gains = refs[6 : 6 + n], refs[6 + n : 6 + 2 * n], refs[6 + 2 * n : 6 + 3 * n]
    xn_out, qkv_out, lse_out, o_out, h_out, yn_out, qkv, xn = refs[6 + 3 * n :]
    step = pl.program_id(0)

    @pl.when(step == 0)
    def _():
        unit, _ = normal(dot(u[...], order[...]))
        xn[...] = (unit * gain_rows(gains)[0:1]).astype(BF)
        xn_out[...] = xn[...]

    packed = dot(xn[...], stack_rows(proj))

    @pl.when(step < steps * 2 // 3)
    def _():
        turned = packed * widen(cos[...], ATTN_TILE) + partner(packed) * widen(sin[...], ATTN_TILE)
        qkv[step] = turned.astype(BF)

    @pl.when(step >= steps * 2 // 3)
    def _():
        qkv[step] = packed.astype(BF)

    qkv_out[0] = qkv[step]

    @pl.when(step == steps - 1)
    def _():
        slots = u.shape[0] // micro
        lane = lax.broadcasted_iota(jnp.int32, (slots, 128), 1)
        blocks = []
        for m in range(micro):
            rows = slice(m * slots, (m + 1) * slots)
            bias = pair_bias(col[rows], row[m])
            log_all = jnp.zeros((slots, 128), F32)
            heads = []
            for low in range(0, HEADS, GROUP):
                group = range(low, low + GROUP)
                scores = [contract_last(head_of(qkv, 0, k, rows), head_of(qkv, 1, k, rows)) * SCALE + bias for k in group]
                peaks = [jnp.max(x, -1, keepdims=True) for x in scores]
                scores = [jnp.exp(x - p) for x, p in zip(scores, peaks)]
                totals = [jnp.sum(x, -1, keepdims=True) for x in scores]
                for k, p, t in zip(group, peaks, totals):
                    log_all = jnp.where(lane == k, p + jnp.log(t), log_all)
                probs = [(x * (1.0 / t)).astype(BF) for x, t in zip(scores, totals)]
                heads += [dot(x, head_of(qkv, 2, k, rows)).astype(BF) for k, x in zip(group, probs)]
            lse_out[rows] = log_all
            blocks.append(jnp.concatenate(heads, 1))
        attended = dot(jnp.concatenate(blocks, 0), order[...]).astype(BF)
        o_out[...] = attended
        hidden = u[...].astype(F32) + dot(attended, stack_rows(out))
        h_out[...] = hidden
        unit, _ = normal(hidden)
        gain = contract_last(gain_rows(gains).astype(BF), order[...])[1:2]
        yn_out[...] = dot((unit * gain).astype(BF), order[...]).astype(BF)


def mlp_forward_kernel(n, steps, *refs):
    yn, h, order = refs[:3]
    gate, up, down = refs[3 : 3 + n], refs[3 + n : 3 + 2 * n], refs[3 + 2 * n : -5]
    mid_out, one_out, two_out, z_out, total = refs[-5:]
    step = pl.program_id(0)
    g = dot(yn[...], stack_rows(gate))
    v = dot(yn[...], stack_rows(up))
    cdf = 0.5 * (1.0 + lax.erf(g * math.sqrt(0.5)))
    slope = cdf + g * jnp.exp(-0.5 * g * g) * (1.0 / math.sqrt(2.0 * math.pi))
    unit = g * cdf
    mid = (unit * v).astype(BF)
    mid_out[...] = mid
    one_out[...] = (v * slope).astype(BF)
    two_out[...] = unit.astype(BF)
    part = contract_last(mid, stack_rows(down))

    @pl.when(step == 0)
    def _():
        total[...] = part

    @pl.when(step > 0)
    def _():
        total[...] += part

    @pl.when(step == steps - 1)
    def _():
        z_out[...] = (h[...] + to_absolute(total[...], order[...])).astype(BF)


def mlp_backward_kernel(n, steps, *refs):
    dzr, dz, h, order, one, two = refs[:6]
    gains, gate, up, down = (refs[6 + k * n : 6 + (k + 1) * n] for k in range(4))
    dg_out, dv_out, dh_out, da_out, term_out, total = refs[6 + 4 * n :]
    step = pl.program_id(0)

    @pl.when(step == 0)
    def _():
        total[...] = jnp.zeros_like(total)

    dmid = dot(dzr[...], stack_rows(down))
    dg = (dmid * one[...].astype(F32)).astype(BF)
    dv = (dmid * two[...].astype(F32)).astype(BF)
    dg_out[...] = dg
    dv_out[...] = dv
    total[...] += contract_last(dg, stack_rows(gate)) + contract_last(dv, stack_rows(up))

    @pl.when(step == steps - 1)
    def _():
        dyn = to_absolute(total[...], order[...])
        unit, scale = normal(h[...])
        gain = contract_last(gain_rows(gains).astype(BF), order[...])[1:2]
        term_out[...] = dot((dyn * unit).astype(BF), order[...]).astype(BF)
        dh = dz[...].astype(F32) + normal_back(dyn * gain, unit, scale)
        dh_out[...] = dh
        da_out[...] = dh.astype(BF)


def heads_backward_kernel(n, micro, *refs):
    da, order, cos, sin, col, row, qkv, lse = refs[:8]
    out, dqkv = refs[8 : 8 + n], refs[8 + n]
    tokens, width = da.shape
    rel = contract_last(da[...], stack_rows(out)).astype(BF)
    do_all = contract_last(rel, order[...]).astype(BF)
    slots = tokens // micro
    for m in range(micro):
        at = slice(m * slots, (m + 1) * slots)
        bias = pair_bias(col[at], row[m])
        log_all = lse[at]
        cosine, sine = widen(cos[at], width), widen(sin[at], width)
        dqs, dks, dvs = [], [], []
        for low in range(0, HEADS, GROUP):
            group = range(low, low + GROUP)
            qs, ks, vs = ([head_of(qkv, part, k, at) for k in group] for part in range(3))
            ds = [do_all[at, k * HEAD_DIM : (k + 1) * HEAD_DIM] for k in group]
            probs = [contract_last(q, k) * SCALE + bias for q, k in zip(qs, ks)]
            probs = [jnp.exp(x - log_all[:, k : k + 1]) for x, k in zip(probs, group)]
            dps = [contract_last(d, v) for d, v in zip(ds, vs)]
            dss = [(p * (x - jnp.sum(p * x, -1, keepdims=True))).astype(BF) for p, x in zip(probs, dps)]
            dvs += [contract_first(p.astype(BF), d) for p, d in zip(probs, ds)]
            dqs += [dot(x, k) for x, k in zip(dss, ks)]
            dks += [contract_first(x, q) for x, q in zip(dss, qs)]
        dq, dk = (jnp.concatenate(x, 1) * SCALE for x in (dqs, dks))
        dqkv[at, :width] = (dq * cosine - partner(dq) * sine).astype(BF)
        dqkv[at, width : 2 * width] = (dk * cosine - partner(dk) * sine).astype(BF)
        dqkv[at, 2 * width :] = jnp.concatenate(dvs, 1).astype(BF)


def qkv_backward_kernel(n, steps, *refs):
    dqkv, dh, u, order = refs[:4]
    gains, proj = refs[4 : 4 + n], refs[4 + n : 4 + 2 * n]
    du_out, term_out, total = refs[4 + 2 * n :]
    step = pl.program_id(0)

    @pl.when(step == 0)
    def _():
        total[...] = jnp.zeros_like(total)

    total[...] += contract_last(dqkv[...], stack_rows(proj))

    @pl.when(step == steps - 1)
    def _():
        unit, scale = normal(dot(u[...], order[...]))
        dxn = total[...]
        term_out[...] = (dxn * unit).astype(BF)
        back = normal_back(dxn * gain_rows(gains)[0:1], unit, scale)
        du_out[...] = (dh[...] + to_absolute(back, order[...])).astype(BF)


def columns(pieces, tile, place):
    return [pl.BlockSpec((p.shape[0], tile), lambda j: (0, place(j))) for p in pieces]


def whole(array):
    return pl.BlockSpec(array.shape, lambda j: (0,) * array.ndim)


def shape_of(rows, cols, kind=BF):
    return jax.ShapeDtypeStruct((rows, cols), kind)


def fixed(rows, cols):
    return pl.BlockSpec((rows, cols), lambda j: (0, 0))


def tiled(rows, cols, start=0, count=None):
    if count is None:
        return pl.BlockSpec((rows, cols), lambda j: (0, j))
    return pl.BlockSpec((rows, cols), lambda j: (0, jnp.clip(j - start, 0, count - 1)))


def cost(flops, weights):
    return pl.CostEstimate(flops=int(flops) // 64, bytes_accessed=int(weights * 2) // 64, transcendentals=0)


def attn_forward(u, pieces, common):
    order, cos, sin, col, row = common
    n, (tokens, width) = len(pieces), u.shape
    steps = 3 * width // ATTN_TILE
    args = (u, *common)
    return pl.pallas_call(
        functools.partial(attn_forward_kernel, n, row.shape[0], steps),
        grid=(steps,),
        in_specs=[whole(a) for a in args]
        + columns(pieces, ATTN_TILE, lambda j: j)
        + columns(pieces, width, lambda j: 3)
        + columns(pieces, 128, lambda j: 4 * width // 128),
        out_specs=[
            fixed(tokens, width),
            pl.BlockSpec((1, tokens, ATTN_TILE), lambda j: (j, 0, 0)),
            fixed(tokens, 128),
            fixed(tokens, width),
            fixed(tokens, width),
            fixed(tokens, width),
        ],
        out_shape=[
            shape_of(tokens, width),
            jax.ShapeDtypeStruct((steps, tokens, ATTN_TILE), BF),
            shape_of(tokens, 128, F32),
            shape_of(tokens, width),
            shape_of(tokens, width, F32),
            shape_of(tokens, width),
        ],
        scratch_shapes=[pltpu.VMEM((steps, tokens, ATTN_TILE), BF), pltpu.VMEM((tokens, width), BF)],
        compiler_params=PARAMS,
        cost_estimate=cost(2 * tokens * 6 * width * width, 5 * width * width),
    )(*args, *pieces, *pieces, *pieces)


def mlp_forward(yn, h, pieces, order):
    n, (tokens, width) = len(pieces), yn.shape
    hidden = pieces[0].shape[1] // 3
    steps = hidden // MLP_TILE
    args = (yn, h, order)
    return pl.pallas_call(
        functools.partial(mlp_forward_kernel, n, steps),
        grid=(steps,),
        in_specs=[whole(a) for a in args]
        + columns(pieces, MLP_TILE, lambda j: j)
        + columns(pieces, MLP_TILE, lambda j: steps + j)
        + columns(pieces, MLP_TILE, lambda j: 2 * steps + j),
        out_specs=[tiled(tokens, MLP_TILE)] * 3 + [fixed(tokens, width)],
        out_shape=[shape_of(tokens, hidden)] * 3 + [shape_of(tokens, width)],
        scratch_shapes=[pltpu.VMEM((tokens, width), F32)],
        compiler_params=PARAMS,
        cost_estimate=cost(6 * tokens * hidden * width, 4 * hidden * width),
    )(*args, *pieces, *pieces, *pieces)


def mlp_backward(dzr, dz, h, one, two, pieces_a, pieces, order):
    n, (tokens, width) = len(pieces), dz.shape
    hidden = pieces[0].shape[1] // 3
    steps = hidden // MLP_TILE
    args = (dzr, dz, h, order)
    return pl.pallas_call(
        functools.partial(mlp_backward_kernel, n, steps),
        grid=(steps,),
        in_specs=[whole(a) for a in args]
        + [tiled(tokens, MLP_TILE)] * 2
        + columns(pieces_a, 128, lambda j: 4 * width // 128)
        + columns(pieces, MLP_TILE, lambda j: j)
        + columns(pieces, MLP_TILE, lambda j: steps + j)
        + columns(pieces, MLP_TILE, lambda j: 2 * steps + j),
        out_specs=[tiled(tokens, MLP_TILE)] * 2 + [fixed(tokens, width)] * 3,
        out_shape=[shape_of(tokens, hidden)] * 2
        + [shape_of(tokens, width, F32), shape_of(tokens, width), shape_of(tokens, width)],
        scratch_shapes=[pltpu.VMEM((tokens, width), F32)],
        compiler_params=PARAMS,
        cost_estimate=cost(6 * tokens * hidden * width, 4 * hidden * width),
    )(*args, one, two, *pieces_a, *pieces, *pieces, *pieces)


def heads_backward(da, common, qkv, lse, pieces):
    n, (tokens, width) = len(pieces), da.shape
    args = (da, *common, qkv, lse)
    return pl.pallas_call(
        functools.partial(heads_backward_kernel, n, common[-1].shape[0]),
        grid=(1,),
        in_specs=[whole(a) for a in args] + columns(pieces, width, lambda j: 3),
        out_specs=fixed(tokens, 3 * width),
        out_shape=shape_of(tokens, 3 * width),
        compiler_params=PARAMS,
        cost_estimate=cost(2 * tokens * width * width, width * width),
    )(*args, *pieces)


def qkv_backward(dqkv, dh, u, order, pieces):
    n, (tokens, width) = len(pieces), u.shape
    steps = 3 * width // ATTN_TILE
    args = (dh, u, order)
    return pl.pallas_call(
        functools.partial(qkv_backward_kernel, n, steps),
        grid=(steps,),
        in_specs=[tiled(tokens, ATTN_TILE)]
        + [whole(a) for a in args]
        + columns(pieces, 128, lambda j: 4 * width // 128)
        + columns(pieces, ATTN_TILE, lambda j: j),
        out_specs=[fixed(tokens, width), fixed(tokens, width)],
        out_shape=[shape_of(tokens, width), shape_of(tokens, width)],
        scratch_shapes=[pltpu.VMEM((tokens, width), F32)],
        compiler_params=PARAMS,
        cost_estimate=cost(2 * tokens * 3 * width * width, 3 * width * width),
    )(dqkv, *args, *pieces, *pieces)


def product_kernel(counts, sides, *refs):
    count = len(counts)
    lefts, rights, rest = refs[: count + sides], refs[count + sides : 2 * (count + sides)], refs[2 * (count + sides) :]
    outs, turned = rest[:-1], rest[-1]
    step = pl.program_id(0)

    @pl.when(step == 0)
    def _():
        for k, left in enumerate(lefts):
            turned[k] = left[...].T

    begin = 0
    for which in range(count):

        @pl.when((step >= begin) & (step < begin + counts[which]))
        def _(which=which):
            value = dot(turned[which], rights[which][...])
            if sides:
                beside = sum(dot(turned[k], rights[k][...]) for k in range(count, count + sides))
                value = jnp.concatenate([value, beside], 1)
            low = 0
            for out in outs:
                out[...] = value[low : low + out.shape[0]].astype(BF)
                low += out.shape[0]

        begin += counts[which]


def make_product(lefts, rights, tile, side_lefts=(), side_rights=()):
    tokens, width = lefts[0].shape
    counts = [r.shape[1] // tile for r in rights]
    steps = sum(counts)
    starts = [sum(counts[:k]) for k in range(len(counts))]
    every = (*lefts, *side_lefts)
    side = side_rights[0].shape[1] // steps if side_rights else 0
    out_tile = tile + side

    def product(part, sizes):
        span = sum(sizes)
        return pl.pallas_call(
            functools.partial(product_kernel, counts, len(side_lefts)),
            grid=(steps,),
            in_specs=[pl.BlockSpec((tokens, span), lambda j: (0, part)) for _ in every]
            + [tiled(tokens, tile, s, c) for s, c in zip(starts, counts)]
            + [tiled(tokens, side) for _ in side_rights],
            out_specs=[tiled(r, out_tile) for r in sizes],
            out_shape=[shape_of(r, steps * out_tile) for r in sizes],
            scratch_shapes=[pltpu.VMEM((len(every), span, tokens), BF)],
            compiler_params=PARAMS,
            cost_estimate=cost(2 * tokens * span * steps * out_tile, span * steps * out_tile),
        )(*every, *rights, *side_rights)

    return product


def shards(tokens_in, attn_proj, attn_out, mlp_in, mlp_out, gain_attn, gain_mlp, lengths, cotangent):
    section = lax.axis_index("section")
    micro, slots, width = tokens_in.shape
    tokens = micro * slots
    three, hidden = attn_proj.shape[2], mlp_out.shape[2]
    padded = -(-hidden // MLP_TILE) * MLP_TILE
    gains = jnp.zeros((gain_attn.shape[1], GAIN_TILE), BF)
    gains = gains.at[:, 0].set(gain_attn[0]).at[:, 1].set(gain_mlp[0])
    gap = jnp.zeros((gain_attn.shape[1], padded - hidden), BF)
    pieces_a, pieces_m = gather(
        jnp.concatenate([attn_proj[0], attn_out[0], gains], 1),
        jnp.concatenate([mlp_in[0, :, :hidden], gap, mlp_in[0, :, hidden:], gap, mlp_out[0], gap], 1),
    )
    order = relative_order(lax.axis_index("fsdp"))
    base = jnp.where(section == 0, 10000.0, 160000.0).astype(F32)
    reach = jnp.where(section == 0, WINDOW / 2.0, 4.0 * slots).astype(F32)
    segment, inner = segment_info(lengths[:, 0], slots)
    half = HEAD_DIM // 2
    freqs = jnp.exp(-jnp.log(base) * (jnp.arange(half, dtype=F32) * (2.0 / HEAD_DIM)))
    angles = jnp.tile(inner.reshape(tokens, 1).astype(F32) * freqs, (1, 128 // half))
    col = jnp.stack([segment.reshape(tokens).astype(F32), inner.reshape(tokens).astype(F32)], 1)
    col = jnp.concatenate([col, jnp.broadcast_to(reach, (tokens, 126))], 1)
    row = jnp.stack([segment, inner] + [inner] * 6, 1).astype(F32)
    common = (order, jnp.cos(angles), jnp.sin(angles), col, row)

    first_in = tokens_in.reshape(tokens, width)
    _, _, _, _, hid, yn = attn_forward(first_in, pieces_a, common)
    m_block, m_near, m_near2 = pieces_m
    m_near, m_near2, yn = tie(m_near, m_near2, yn)
    m_far, m_far2 = far(m_near, m_near2)
    near_core = core(m_block, m_near, m_near2)
    far_core = core(m_far, m_far2)
    pieces_m = (m_block, m_near, m_far, m_far2, m_near2, *near_core[:2], *far_core, near_core[2])
    middle_out = mlp_forward(yn, hid, pieces_m, order)[3]
    received = lax.ppermute(middle_out, "section", [(0, 1)])
    layer_in = jnp.where(section == 0, first_in, received)
    xn, qkv, lse, attended, hid, yn = attn_forward(layer_in, pieces_a, common)
    mid, one, two, result = mlp_forward(yn, hid, pieces_m, order)

    def backward_mlp(grad):
        rel = dot(grad, order).astype(BF)
        return mlp_backward(rel, grad, hid, one, two, pieces_a, pieces_m, order)

    last_grad = cotangent.reshape(tokens, width)
    _, _, dh, da, _ = backward_mlp(last_grad)
    dqkv = heads_backward(da, common, qkv, lse, pieces_a)
    middle_grad = qkv_backward(dqkv, dh, layer_in, order, pieces_a)[0]
    received = lax.ppermute(middle_grad, "section", [(1, 0)])
    grad_out = jnp.where(section == 1, last_grad, received)
    half = width // 2
    dzr = dot(grad_out, order).astype(BF)
    dg, dv, dh, da, term_m = mlp_backward(dzr, grad_out, hid, one, two, pieces_a, pieces_m, order)
    product = make_product((yn, yn, dzr), (dg, dv, mid), MLP_TILE)
    sent_m, yn = tie(product(1, (half,))[0], yn)
    got_m = send(sent_m, "core")
    product = make_product((yn, yn, dzr), (dg, dv, mid), MLP_TILE)
    own_m = product(0, cut(half))
    here_m, after_m, far_m, far_m2, before_m = ring_start(own_m, got_m)
    far_m, far_m2 = send(far_m.astype(BF), "first", 1), send(far_m2.astype(BF), "first", -1)
    dqkv = heads_backward(da, common, qkv, lse, pieces_a)
    far_m, far_m2, dqkv = tie(far_m, far_m2, dqkv)
    *mix_m, dqkv = tie(*ring_mix(after_m, before_m, far_m, far_m2), dqkv)
    near_m = send(mix_m[0], "first", 1), send(mix_m[1], "first", -1)
    grad_in, term_a = qkv_backward(dqkv, dh, layer_in, order, pieces_a)
    lane = lax.broadcasted_iota(jnp.int32, (tokens, 4 * GAIN_TILE), 1)
    picks = ((lane == 0).astype(BF), (lane == 1).astype(BF))
    product = make_product((xn, attended), (dqkv, da), width, (term_a, term_m), picks)
    *own_a, sent_a = product(0, (*cut(half), half))
    got_a = send(sent_a, "core")
    here_a, after_a, far_a, far_a2, before_a = ring_start(own_a, got_a)
    ends_m = direct(ring_close(here_m, *near_m))
    far_a, far_a2 = send(far_a.astype(BF), "first", 1), send(far_a2.astype(BF), "first", -1)
    mix_a = ring_mix(after_a, before_a, far_a, far_a2)
    *ends_m, mix_a, mix_a2 = tie(*ends_m, *mix_a)
    near_a = send(mix_a, "first", 1), send(mix_a2, "first", -1)
    sum_m = close_z(*ends_m)
    sum_a = close_z(*direct(ring_close(here_a, *near_a)))
    edge = width + GAIN_TILE
    grad_proj = jnp.concatenate([sum_a[:, k * edge : k * edge + width] for k in range(3)], 1)
    grad_up = jnp.concatenate([sum_m[:, :hidden], sum_m[:, padded : padded + hidden]], 1)
    return (
        result.reshape(1, micro, slots, width),
        grad_in.reshape(1, micro, slots, width),
        grad_proj[None],
        sum_a[:, 3 * edge : 3 * edge + width][None],
        grad_up[None],
        sum_m[:, 2 * padded : 2 * padded + hidden][None],
        sum_a[:, width][None],
        sum_a[:, width + 1][None],
    )


def solution(mesh):
    in_specs = (
        P(None, "fsdp", None),
        P("section", "fsdp", None),
        P("section", "fsdp", None),
        P("section", "fsdp", None),
        P("section", "fsdp", None),
        P("section", "fsdp"),
        P("section", "fsdp"),
        P(None, "fsdp", None),
        P(None, "fsdp", None),
    )
    out_specs = (
        P("section", None, "fsdp", None),
        P("section", None, "fsdp", None),
        P("section", "fsdp", None),
        P("section", "fsdp", None),
        P("section", "fsdp", None),
        P("section", "fsdp", None),
        P("section", "fsdp"),
        P("section", "fsdp"),
    )
    return jax.shard_map(shards, mesh=mesh, in_specs=in_specs, out_specs=out_specs, check_vma=False)
```

profile of v0, /device:TPU:8, one launch (start us, length us, event | category | flops | bytes accessed | tf_op | source)
XLA Modules:
  0.0 386.6 jit_solution(12710779268213454456)
XLA Ops:
  32.3 10.4 %collective-permute-done.9 = bf16[32,8064]{1,0:T(8,128)(2,1)S(1)} collective-permute-done((bf16[32,8064]{1,0:T(8,128)(2,1)S(1)}, bf16[32,8064]{1,0:T(8,128)(2,1)S(1)}, u32[]{:S(2)}, u32[]{:S(2)}) %collective-permute-start.9) | collective-permute-done | bytes 516128 | tf_op jit(solution)/shard_map/ppermute | solution.py:51
  46.1 4.4 %collective-permute-done.5.refs_7_.refs_17_.refs_27_.refs_9_.refs_5_.refs_15_ = bf16[128,4224]{1,0:T(8,128)(2,1)S(1)} collective-permute-done((bf16[128,4224]{1,0:T(8,128)(2,1)}, bf16[128,4224]{1,0:T(8,128)(2,1)S(1)}, u32[]{:S(2)}, u32[]{:S(2)}) %collective-permute-start.5) | collective-permute-done | bytes 1081376 | tf_op jit(solution)/shard_map/ppermute | solution.py:51
  53.8 6.3 %collective-permute-done.6.refs_8_.refs_18_.refs_28_.refs_10_.refs_6_.refs_16_ = bf16[64,4224]{1,0:T(8,128)(2,1)} collective-permute-done((bf16[64,4224]{1,0:T(8,128)(2,1)S(1)}, bf16[64,4224]{1,0:T(8,128)(2,1)}, u32[]{:S(2)}, u32[]{:S(2)}) %collective-permute-start.6) | collective-permute-done | bytes 540704 | tf_op jit(solution)/shard_map/ppermute | solution.py:51
  69.1 4.2 %collective-permute-done.16.refs_13_.refs_23_.refs_33_.refs_15_.refs_11_.refs_21_ = bf16[64,4224]{1,0:T(8,128)(2,1)} collective-permute-done((bf16[64,4224]{1,0:T(8,128)(2,1)}, bf16[64,4224]{1,0:T(8,128)(2,1)}, u32[]{:S(2)}, u32[]{:S(2)}) %collective-permute-start.16) | collective-permute-done | bytes 540704 | tf_op jit(solution)/shard_map/ppermute | solution.py:51
  79.6 13.9 %shard_map.152 = (bf16[192,1024]{1,0:T(8,128)(2,1)}, bf16[3,192,1024]{2,1,0:T(8,128)(2,1)}, f32[192,128]{1,0:T(8,128)}, bf16[192,1024]{1,0:T(8,128)(2,1)}, f32[1...) custom-call(bf16[192,1024]{1,0:T(8,128)(2,1)} %bitcast.43, bf16[1024,1024]{1,0:T(8,128)(2,1)} %fusion.2.refs_1_.refs_2_.refs_3_, ...), custom_call_target="tpu_custom_call" | custom-call | flops 37748736 | bytes 163840 | tf_op jit(solution)/shard_map/pallas_call | solution.py:413
  98.6 9.8 %collective-permute-done.19.refs_5_.refs_15_.refs_25_.refs_18_.refs_28_.refs_38_ = bf16[64,8064]{1,0:T(8,128)(2,1)S(1)} collective-permute-done((bf16[64,8064]{1,0:T(8,128)(2,1)S(1)}, bf16[64,8064]{1,0:T(8,128)(2,1)S(1)}, u32[]{:S(2)}, u32[]{:S(2)}) %collective-permute-start.19) | collective-permute-done | bytes 1032224 | tf_op jit(solution)/shard_map/ppermute | solution.py:51
  116.9 13.3 %shard_map.153 = (bf16[192,2688]{1,0:T(8,128)(2,1)}, bf16[192,2688]{1,0:T(8,128)(2,1)}, bf16[192,2688]{1,0:T(8,128)(2,1)}, bf16[192,1024]{1,0:T(8,128)(2,1)}) custom-call(bf16[192,1024]{1,0:T(8,128)(2,1)} %get-tuple-element.98.refs_0_, f32[192,1024]{1,0:T(8,128)} %get-tuple-element.99.refs_1_, bf16[1024,1024]{1,0:T(8,128)(2,1)} %fusion.2.refs_1_.refs_2_.refs_3_, ...), custom_call_target="tpu_custom_call" | custom-call | flops 49545216 | bytes 344064 | tf_op jit(solution)/shard_map/pallas_call | solution.py:447
  130.2 5.6 %collective-permute-start.26 = (bf16[192,1024]{1,0:T(8,128)(2,1)}, bf16[192,1024]{1,0:T(8,128)(2,1)S(1)}, u32[]{:S(2)}, u32[]{:S(2)}) collective-permute-start(bf16[192,1024]{1,0:T(8,128)(2,1)} %get-tuple-element.102), channel_id=1, source_target_pairs={{0,64},{1,65},{2,66},{3,67},{4,68},{5,69},{6,70},{7,71},{8,72},{9,... | collective-permute-start | bytes 1179656 | tf_op jit(solution)/shard_map/ppermute | solution.py:607
  137.5 7.5 %collective-permute-done.26 = bf16[192,1024]{1,0:T(8,128)(2,1)S(1)} collective-permute-done((bf16[192,1024]{1,0:T(8,128)(2,1)}, bf16[192,1024]{1,0:T(8,128)(2,1)S(1)}, u32[]{:S(2)}, u32[]{:S(2)}) %collective-permute-start.26) | collective-permute-done | bytes 393248 | tf_op jit(solution)/shard_map/ppermute | solution.py:607
  145.8 14.3 %shard_map.154 = (bf16[192,1024]{1,0:T(8,128)(2,1)}, bf16[3,192,1024]{2,1,0:T(8,128)(2,1)}, f32[192,128]{1,0:T(8,128)}, bf16[192,1024]{1,0:T(8,128)(2,1)}, f32[1...) custom-call(bf16[192,1024]{1,0:T(8,128)(2,1)} %broadcast_select_fusion.1.refs_0_.refs_2_, ...), custom_call_target="tpu_custom_call" | custom-call | flops 37748736 | bytes 163840 | tf_op jit(solution)/shard_map/pallas_call | solution.py:413
  160.1 13.3 %shard_map.155 = (bf16[192,2688]{1,0:T(8,128)(2,1)}, bf16[192,2688]{1,0:T(8,128)(2,1)}, bf16[192,2688]{1,0:T(8,128)(2,1)}, bf16[192,1024]{1,0:T(8,128)(2,1)}) custom-call(bf16[192,1024]{1,0:T(8,128)(2,1)} %get-tuple-element.116.refs_0_.refs_1_, f32[192,1024]{1,0:T(8,128)} %get-tuple-element.104.refs_1_.refs_2_, ...), custom_call_target="tpu_custom_call" | custom-call | flops 49545216 | bytes 344064 | tf_op jit(solution)/shard_map/pallas_call | solution.py:447
  173.5 15.5 %shard_map.156 = (bf16[192,2688]{1,0:T(8,128)(2,1)}, bf16[192,2688]{1,0:T(8,128)(2,1)}, f32[192,1024]{1,0:T(8,128)}, bf16[192,1024]{1,0:T(8,128)(2,1)}, bf16[192,1024]{1,0:T(8,128)(2,1)}) custom-call(bf16[192,1024]{1,0:T(8,128)(2,1)} %fusion.9.refs_0_, bf16[192,1024]{1,0:T(8,128)(2,1)} %bitcast.44, f32[192,1024]{1,0:T(8,128)} %get-tuple-element.104.refs_1_.refs_2_, ...), custom_call_target="tpu_custom_call" | custom-call | flops 49545216 | bytes 344064 | tf_op jit(solution)/shard_map/pallas_call | solution.py:467
  189.0 8.8 %shard_map.157.refs_0_ = bf16[192,3072]{1,0:T(8,128)(2,1)} custom-call(bf16[192,1024]{1,0:T(8,128)(2,1)} %get-tuple-element.108.refs_0_, bf16[1024,1024]{1,0:T(8,128)(2,1)} %fusion.2.refs_1_.refs_2_.refs_3_, f32[192,128]{1,0:T(8,128)} %copy.51.refs_2_, f32[192,128]{1,0:T(8,128)} %copy.52.refs_3_, f32[192,128]{1,0:T(8,128)} %maximum_maximum_fusion.refs_4_, ...), custom_call_target="tpu_custom_call" | custom-call | flops 6291456 | bytes 32768 | tf_op jit(solution)/shard_map/pallas_call | solution.py:488
  197.8 9.7 %shard_map.158 = (bf16[192,1024]{1,0:T(8,128)(2,1)}, bf16[192,1024]{1,0:T(8,128)(2,1)}) custom-call(bf16[192,3072]{1,0:T(8,128)(2,1)} %shard_map.157.refs_0_, f32[192,1024]{1,0:T(8,128)} %get-tuple-element.111.refs_1_, bf16[192,1024]{1,0:T(8,128)(2,1)} %broadcast_select_fusion.1.refs_0_.refs_2_, bf16[1024,1024]{1,0:T(8,128)(2,1)} %fusion.2.refs_1_.refs_2_.refs_3_, ...), custom_call_target="tpu_custom_call" | custom-call | flops 18874368 | bytes 98304 | tf_op jit(solution)/shard_map/pallas_call | solution.py:503
  208.8 12.9 %collective-permute-done.27 = bf16[192,1024]{1,0:T(8,128)(2,1)S(1)} collective-permute-done((bf16[192,1024]{1,0:T(8,128)(2,1)}, bf16[192,1024]{1,0:T(8,128)(2,1)S(1)}, u32[]{:S(2)}, u32[]{:S(2)}) %collective-permute-start.27) | collective-permute-done | bytes 393248 | tf_op jit(solution)/shard_map/ppermute | solution.py:620
  223.5 15.5 %shard_map.159 = (bf16[192,2688]{1,0:T(8,128)(2,1)}, bf16[192,2688]{1,0:T(8,128)(2,1)}, f32[192,1024]{1,0:T(8,128)}, bf16[192,1024]{1,0:T(8,128)(2,1)}, bf16[192,1024]{1,0:T(8,128)(2,1)}) custom-call(bf16[192,1024]{1,0:T(8,128)(2,1)} %fusion.8.refs_0_.refs_2_, bf16[192,1024]{1,0:T(8,128)(2,1)} %copy-done.14, f32[192,1024]{1,0:T(8,128)} %get-tuple-element.104.refs_1_.refs_2_, ...), custom_call_target="tpu_custom_call" | custom-call | flops 49545216 | bytes 344064 | tf_op jit(solution)/shard_map/pallas_call | solution.py:467
  239.0 9.7 %shard_map.160 = bf16[512,8064]{1,0:T(8,128)(2,1)} custom-call(bf16[192,1024]{1,0:T(8,128)(2,1)} %get-tuple-element.116.refs_0_.refs_1_, bf16[192,1024]{1,0:T(8,128)(2,1)} %get-tuple-element.116.refs_0_.refs_1_, bf16[192,1024]{1,0:T(8,128)(2,1)} %fusion.8.refs_0_.refs_2_, bf16[192,2688]{1,0:T(8,128)(2,1)} %get-tuple-element.113.refs_3_, ...), custom_call_target="tpu_custom_call" | custom-call | flops 24772608 | bytes 129024 | tf_op jit(solution)/shard_map/pallas_call | solution.py:557
  248.7 8.9 %shard_map.162.refs_0_.refs_4_ = bf16[192,3072]{1,0:T(8,128)(2,1)} custom-call(bf16[192,1024]{1,0:T(8,128)(2,1)} %get-tuple-element.121.refs_0_.refs_5_, bf16[1024,1024]{1,0:T(8,128)(2,1)} %fusion.2.refs_1_.refs_2_.refs_3_, f32[192,128]{1,0:T(8,128)} %copy.51.refs_2_, f32[192,128]{1,0:T(8,128)} %copy.52.refs_3_, f32[192,128]{1,0:T(8,128)} %maximum_maximum_fusion.refs_4_, ...), custom_call_target="tpu_custom_call" | custom-call | flops 6291456 | bytes 32768 | tf_op jit(solution)/shard_map/pallas_call | solution.py:488
  257.6 9.7 %shard_map.161 = (bf16[128,8064]{1,0:T(8,128)(2,1)}, bf16[128,8064]{1,0:T(8,128)(2,1)}, bf16[64,8064]{1,0:T(8,128)(2,1)}, bf16[64,8064]{1,0:T(8,128)(2,1)}, bf16[128,8064]{1,0:T(8,128)(2,1)}) custom-call(bf16[192,1024]{1,0:T(8,128)(2,1)} %get-tuple-element.116.refs_0_.refs_1_, bf16[192,1024]{1,0:T(8,128)(2,1)} %get-tuple-element.116.refs_0_.refs_1_, ...), custom_call_target="tpu_custom_call" | custom-call | flops 24772608 | bytes 129024 | tf_op jit(solution)/shard_map/pallas_call | solution.py:557
  273.0 11.1 %collective-permute-done.29 = bf16[64,8064]{1,0:T(8,128)(2,1)S(1)} collective-permute-done((bf16[64,8064]{1,0:T(8,128)(2,1)S(1)}, bf16[64,8064]{1,0:T(8,128)(2,1)S(1)}, u32[]{:S(2)}, u32[]{:S(2)}) %collective-permute-start.29) | collective-permute-done | bytes 1032224 | tf_op jit(solution)/shard_map/ppermute | solution.py:51
  292.1 9.6 %shard_map.163 = (bf16[192,1024]{1,0:T(8,128)(2,1)}, bf16[192,1024]{1,0:T(8,128)(2,1)}) custom-call(bf16[192,3072]{1,0:T(8,128)(2,1)} %shard_map.162.refs_0_.refs_4_, f32[192,1024]{1,0:T(8,128)} %get-tuple-element.127.refs_1_, bf16[192,1024]{1,0:T(8,128)(2,1)} %broadcast_select_fusion.1.refs_0_.refs_2_, bf16[1024,1024]{1,0:T(8,128)(2,1)} %fusion.2.refs_1_.refs_2_.refs_3_, ...), custom_call_target="tpu_custom_call" | custom-call | flops 18874368 | bytes 98304 | tf_op jit(solution)/shard_map/pallas_call | solution.py:503
  303.1 8.4 %shard_map.164 = (bf16[128,4608]{1,0:T(8,128)(2,1)}, bf16[128,4608]{1,0:T(8,128)(2,1)}, bf16[64,4608]{1,0:T(8,128)(2,1)}, bf16[64,4608]{1,0:T(8,128)(2,1)}, bf16...) custom-call(bf16[192,1024]{1,0:T(8,128)(2,1)} %get-tuple-element.129.refs_0_, ...), custom_call_target="tpu_custom_call" | custom-call | flops 28311552 | bytes 147456 | tf_op jit(solution)/shard_map/pallas_call | solution.py:557
  311.8 4.3 %collective-permute-done.32 = bf16[128,8064]{1,0:T(8,128)(2,1)} collective-permute-done((bf16[128,8064]{1,0:T(8,128)(2,1)}, bf16[128,8064]{1,0:T(8,128)(2,1)}, u32[]{:S(2)}, u32[]{:S(2)}) %collective-permute-start.32) | collective-permute-done | bytes 2064416 | tf_op jit(solution)/shard_map/ppermute | solution.py:51
  318.9 3.8 add_convert_fusion
  323.5 3.8 collective-permute-start.35
  330.9 11.4 %collective-permute-done.38 = bf16[64,4608]{1,0:T(8,128)(2,1)S(1)} collective-permute-done((bf16[64,4608]{1,0:T(8,128)(2,1)S(1)}, bf16[64,4608]{1,0:T(8,128)(2,1)S(1)}, u32[]{:S(2)}, u32[]{:S(2)}) %collective-permute-start.38) | collective-permute-done | bytes 589856 | tf_op jit(solution)/shard_map/ppermute | solution.py:51
  342.7 3.4 collective-permute-done.35
  349.6 4.7 %collective-permute-done.45 = bf16[16,8064]{1,0:T(8,128)(2,1)S(1)} collective-permute-done((bf16[16,8064]{1,0:T(8,128)(2,1)S(1)}, bf16[16,8064]{1,0:T(8,128)(2,1)S(1)}, u32[]{:S(2)}, u32[]{:S(2)}) %collective-permute-start.45) | collective-permute-done | bytes 258080 | tf_op jit(solution)/shard_map/ppermute | solution.py:51
  354.4 9.4 %collective-permute-done.39 = bf16[128,4608]{1,0:T(8,128)(2,1)S(1)} collective-permute-done((bf16[128,4608]{1,0:T(8,128)(2,1)S(1)}, bf16[128,4608]{1,0:T(8,128)(2,1)S(1)}, u32[]{:S(2)}, u32[]{:S(2)}) %collective-permute-start.39) | collective-permute-done | bytes 1179680 | tf_op jit(solution)/shard_map/ppermute | solution.py:51
  366.6 3.3 collective-permute-start.42
  370.6 3.9 %collective-permute-done.41 = bf16[32,4608]{1,0:T(8,128)(2,1)S(1)} collective-permute-done((bf16[32,4608]{1,0:T(8,128)(2,1)S(1)}, bf16[32,4608]{1,0:T(8,128)(2,1)S(1)}, u32[]{:S(2)}, u32[]{:S(2)}) %collective-permute-start.41) | collective-permute-done | bytes 294944 | tf_op jit(solution)/shard_map/ppermute | solution.py:51
  380.7 3.3 collective-permute-done.44
  (202 shorter events, 110.7 us)
Async XLA Ops:
  28.0 14.6 %collective-permute-start.9 = (bf16[32,8064]{1,0:T(8,128)(2,1)S(1)}, bf16[32,8064]{1,0:T(8,128)(2,1)S(1)}, u32[]{:S(2)}, u32[]{:S(2)}) collective-permute-start(bf16[32,8064]{1,0:T(8,128)(2,1)S(1)} %get-tuple-element.172), channel_id=1, source_target_pairs={{0,12},{1,49},{2,14},{3,51},{4,0},{5,53},{6,2},{7,55},{8,4},{9,57}... | collective-permute-start | bytes 1548296 | tf_op jit(solution)/shard_map/ppermute | solution.py:51
  29.2 16.1 %collective-permute-start.10 = (bf16[32,8064]{1,0:T(8,128)(2,1)S(1)}, bf16[32,8064]{1,0:T(8,128)(2,1)S(1)}, u32[]{:S(2)}, u32[]{:S(2)}) collective-permute-start(bf16[32,8064]{1,0:T(8,128)(2,1)S(1)} %get-tuple-element.172), channel_id=1, source_target_pairs={{0,8},{1,33},{2,10},{3,35},{4,12},{5,37},{6,14},{7,39},{8,0},{9,41... | collective-permute-start | bytes 1548296 | tf_op jit(solution)/shard_map/ppermute | solution.py:51
  29.4 23.6 %collective-permute-start.11 = (bf16[32,8064]{1,0:T(8,128)(2,1)S(1)}, bf16[32,8064]{1,0:T(8,128)(2,1)S(1)}, u32[]{:S(2)}, u32[]{:S(2)}) collective-permute-start(bf16[32,8064]{1,0:T(8,128)(2,1)S(1)} %get-tuple-element.172), channel_id=1, source_target_pairs={{0,4},{1,17},{2,6},{3,19},{4,8},{5,21},{6,10},{7,23},{8,12},{9,25}... | collective-permute-start | bytes 1548296 | tf_op jit(solution)/shard_map/ppermute | solution.py:51
  30.3 20.3 %collective-permute-start.5 = (bf16[128,4224]{1,0:T(8,128)(2,1)}, bf16[128,4224]{1,0:T(8,128)(2,1)S(1)}, u32[]{:S(2)}, u32[]{:S(2)}) collective-permute-start(bf16[128,4224]{1,0:T(8,128)(2,1)} %constant_dynamic-update-slice_fusion.refs_6_.refs_16_.refs_26_.refs_8_.refs_4_.refs_14_), channel_id=1, source_target_pairs={{0,48},{1,13},{2,50},{3,15},{4,52},{5,1},{6,54},{7,3},{8,56},{9,5}... | collective-permute-start | bytes 3244040 | tf_op jit(solution)/shard_map/ppermute | solution.py:51
  30.7 21.4 %collective-permute-start.7 = (bf16[128,4224]{1,0:T(8,128)(2,1)}, bf16[128,4224]{1,0:T(8,128)(2,1)S(1)}, u32[]{:S(2)}, u32[]{:S(2)}) collective-permute-start(bf16[128,4224]{1,0:T(8,128)(2,1)} %constant_dynamic-update-slice_fusion.refs_6_.refs_16_.refs_26_.refs_8_.refs_4_.refs_14_), channel_id=1, source_target_pairs={{0,16},{1,5},{2,18},{3,7},{4,20},{5,9},{6,22},{7,11},{8,24},{9,13}... | collective-permute-start | bytes 3244040 | tf_op jit(solution)/shard_map/ppermute | solution.py:51
  42.6 25.8 %collective-permute-start.14 = (bf16[128,4224]{1,0:T(8,128)(2,1)}, bf16[128,4224]{1,0:T(8,128)(2,1)}, u32[]{:S(2)}, u32[]{:S(2)}) collective-permute-start(bf16[128,4224]{1,0:T(8,128)(2,1)} %constant_dynamic-update-slice_fusion.refs_6_.refs_16_.refs_26_.refs_8_.refs_4_.refs_14_), channel_id=1, source_target_pairs={{0,1},{1,0},{2,3},{3,2},{4,5},{5,4},{6,7},{7,6},{8,9},{9,8},{10,11... | collective-permute-start | bytes 3244040 | tf_op jit(solution)/shard_map/ppermute | solution.py:51
  52.2 10.9 %collective-permute-start.8 = (bf16[64,4224]{1,0:T(8,128)(2,1)S(1)}, bf16[64,4224]{1,0:T(8,128)(2,1)}, u32[]{:S(2)}, u32[]{:S(2)}) collective-permute-start(bf16[64,4224]{1,0:T(8,128)(2,1)S(1)} %slice.214), channel_id=1, source_target_pairs={{0,16},{1,5},{2,18},{3,7},{4,20},{5,9},{6,22},{7,11},{8,24},{9,13}... | collective-permute-start | bytes 1622024 | tf_op jit(solution)/shard_map/ppermute | solution.py:51
  63.1 30.4 %collective-permute-start.12 = (bf16[128,8064]{1,0:T(8,128)(2,1)}, bf16[128,8064]{1,0:T(8,128)(2,1)S(1)}, u32[]{:S(2)}, u32[]{:S(2)}) collective-permute-start(bf16[128,8064]{1,0:T(8,128)(2,1)} %constant_dynamic-update-slice_fusion.7.refs_3_.refs_13_.refs_23_.refs_16_.refs_26_.refs_36_), channel_id=1, source_target_pairs={{0,48},{1,13},{2,50},{3,15},{4,52},{5,1},{6,54},{7,3},{8,56},{9,5}... | collective-permute-start | bytes 6193160 | tf_op jit(solution)/shard_map/ppermute | solution.py:51
  66.3 27.2 %collective-permute-start.13 = (bf16[128,8064]{1,0:T(8,128)(2,1)}, bf16[128,8064]{1,0:T(8,128)(2,1)}, u32[]{:S(2)}, u32[]{:S(2)}) collective-permute-start(bf16[128,8064]{1,0:T(8,128)(2,1)} %constant_dynamic-update-slice_fusion.7.refs_3_.refs_13_.refs_23_.refs_16_.refs_26_.refs_36_), channel_id=1, source_target_pairs={{0,16},{1,5},{2,18},{3,7},{4,20},{5,9},{6,22},{7,11},{8,24},{9,13}... | collective-permute-start | bytes 6193160 | tf_op jit(solution)/shard_map/ppermute | solution.py:51
  66.7 12.9 %collective-permute-start.15 = (bf16[128,4224]{1,0:T(8,128)(2,1)S(1)}, bf16[128,4224]{1,0:T(8,128)(2,1)}, u32[]{:S(2)}, u32[]{:S(2)}) collective-permute-start(bf16[128,4224]{1,0:T(8,128)(2,1)S(1)} %collective-permute-done.5.refs_7_.refs_17_.refs_27_.refs_9_.refs_5_.refs_15_), channel_id=1, source_target_pairs={{0,1},{1,0},{2,3},{3,2},{4,5},{5,4},{6,7},{7,6},{8,9},{9,8},{10,11... | collective-permute-start | bytes 3244040 | tf_op jit(solution)/shard_map/ppermute | solution.py:51
  68.3 11.3 %collective-permute-start.18 = (bf16[128,4224]{1,0:T(8,128)(2,1)}, bf16[128,4224]{1,0:T(8,128)(2,1)}, u32[]{:S(2)}, u32[]{:S(2)}) collective-permute-start(bf16[128,4224]{1,0:T(8,128)(2,1)} %copy-done.4), channel_id=1, source_target_pairs={{0,1},{1,0},{2,3},{3,2},{4,5},{5,4},{6,7},{7,6},{8,9},{9,8},{10,11... | collective-permute-start | bytes 3244040 | tf_op jit(solution)/shard_map/ppermute | solution.py:51
  79.3 33.7 %collective-permute-start.21 = (bf16[128,8064]{1,0:T(8,128)(2,1)}, bf16[128,8064]{1,0:T(8,128)(2,1)S(1)}, u32[]{:S(2)}, u32[]{:S(2)}) collective-permute-start(bf16[128,8064]{1,0:T(8,128)(2,1)} %constant_dynamic-update-slice_fusion.7.refs_3_.refs_13_.refs_23_.refs_16_.refs_26_.refs_36_), channel_id=1, source_target_pairs={{0,1},{1,0},{2,3},{3,2},{4,5},{5,4},{6,7},{7,6},{8,9},{9,8},{10,11... | collective-permute-start | bytes 6193160 | tf_op jit(solution)/shard_map/ppermute | solution.py:51
  93.6 14.7 %collective-permute-start.19 = (bf16[64,8064]{1,0:T(8,128)(2,1)S(1)}, bf16[64,8064]{1,0:T(8,128)(2,1)S(1)}, u32[]{:S(2)}, u32[]{:S(2)}) collective-permute-start(bf16[64,8064]{1,0:T(8,128)(2,1)S(1)} %slice.172), channel_id=1, source_target_pairs={{0,48},{1,13},{2,50},{3,15},{4,52},{5,1},{6,54},{7,3},{8,56},{9,5}... | collective-permute-start | bytes 3096584 | tf_op jit(solution)/shard_map/ppermute | solution.py:51
  95.9 14.9 %collective-permute-start.20 = (bf16[64,8064]{1,0:T(8,128)(2,1)S(1)}, bf16[64,8064]{1,0:T(8,128)(2,1)S(1)}, u32[]{:S(2)}, u32[]{:S(2)}) collective-permute-start(bf16[64,8064]{1,0:T(8,128)(2,1)S(1)} %slice.173), channel_id=1, source_target_pairs={{0,16},{1,5},{2,18},{3,7},{4,20},{5,9},{6,22},{7,11},{8,24},{9,13}... | collective-permute-start | bytes 3096584 | tf_op jit(solution)/shard_map/ppermute | solution.py:51
  97.2 18.1 %collective-permute-start.22 = (bf16[128,8064]{1,0:T(8,128)(2,1)S(1)}, bf16[128,8064]{1,0:T(8,128)(2,1)S(1)}, u32[]{:S(2)}, u32[]{:S(2)}) collective-permute-start(bf16[128,8064]{1,0:T(8,128)(2,1)S(1)} %collective-permute-done.12.refs_4_.refs_14_.refs_24_.refs_17_.refs_27_.refs_37_), channel_id=1, source_target_pairs={{0,1},{1,0},{2,3},{3,2},{4,5},{5,4},{6,7},{7,6},{8,9},{9,8},{10,11... | collective-permute-start | bytes 6193160 | tf_op jit(solution)/shard_map/ppermute | solution.py:51
  98.5 16.9 %collective-permute-start.25 = (bf16[128,8064]{1,0:T(8,128)(2,1)}, bf16[128,8064]{1,0:T(8,128)(2,1)}, u32[]{:S(2)}, u32[]{:S(2)}) collective-permute-start(bf16[128,8064]{1,0:T(8,128)(2,1)} %collective-permute-done.13.refs_7_.refs_17_.refs_27_.refs_20_.refs_30_.refs_40_), channel_id=1, source_target_pairs={{0,1},{1,0},{2,3},{3,2},{4,5},{5,4},{6,7},{7,6},{8,9},{9,8},{10,11... | collective-permute-start | bytes 6193160 | tf_op jit(solution)/shard_map/ppermute | solution.py:51
  130.2 14.7 %collective-permute-start.26 = (bf16[192,1024]{1,0:T(8,128)(2,1)}, bf16[192,1024]{1,0:T(8,128)(2,1)S(1)}, u32[]{:S(2)}, u32[]{:S(2)}) collective-permute-start(bf16[192,1024]{1,0:T(8,128)(2,1)} %get-tuple-element.102), channel_id=1, source_target_pairs={{0,64},{1,65},{2,66},{3,67},{4,68},{5,69},{6,70},{7,71},{8,72},{9,... | collective-permute-start | bytes 1179656 | tf_op jit(solution)/shard_map/ppermute | solution.py:607
  207.5 14.2 %collective-permute-start.27 = (bf16[192,1024]{1,0:T(8,128)(2,1)}, bf16[192,1024]{1,0:T(8,128)(2,1)S(1)}, u32[]{:S(2)}, u32[]{:S(2)}) collective-permute-start(bf16[192,1024]{1,0:T(8,128)(2,1)} %get-tuple-element.112), channel_id=1, source_target_pairs={{64,0},{65,1},{66,2},{67,3},{68,4},{69,5},{70,6},{71,7},{72,8},{73... | collective-permute-start | bytes 1179656 | tf_op jit(solution)/shard_map/ppermute | solution.py:620
  248.7 18.6 %collective-permute-start.28 = (bf16[512,8064]{1,0:T(8,128)(2,1)}, bf16[512,8064]{1,0:T(8,128)(2,1)S(1)}, u32[]{:S(2)}, u32[]{:S(2)}) collective-permute-start(bf16[512,8064]{1,0:T(8,128)(2,1)} %shard_map.160), channel_id=1, source_target_pairs={{0,1},{1,0},{2,3},{3,2},{4,5},{5,4},{6,7},{7,6},{8,9},{9,8},{10,11... | collective-permute-start | bytes 24772616 | tf_op jit(solution)/shard_map/ppermute | solution.py:51
  269.5 14.7 %collective-permute-start.29 = (bf16[64,8064]{1,0:T(8,128)(2,1)S(1)}, bf16[64,8064]{1,0:T(8,128)(2,1)S(1)}, u32[]{:S(2)}, u32[]{:S(2)}) collective-permute-start(bf16[64,8064]{1,0:T(8,128)(2,1)S(1)} %get-tuple-element.153), channel_id=1, source_target_pairs={{0,16},{1,5},{2,18},{3,7},{4,20},{5,9},{6,22},{7,11},{8,24},{9,13}... | collective-permute-start | bytes 3096584 | tf_op jit(solution)/shard_map/ppermute | solution.py:51
  269.8 15.7 %collective-permute-start.30 = (bf16[64,8064]{1,0:T(8,128)(2,1)S(1)}, bf16[64,8064]{1,0:T(8,128)(2,1)}, u32[]{:S(2)}, u32[]{:S(2)}) collective-permute-start(bf16[64,8064]{1,0:T(8,128)(2,1)S(1)} %get-tuple-element.152), channel_id=1, source_target_pairs={{0,48},{1,13},{2,50},{3,15},{4,52},{5,1},{6,54},{7,3},{8,56},{9,5}... | collective-permute-start | bytes 3096584 | tf_op jit(solution)/shard_map/ppermute | solution.py:51
  290.1 26.0 %collective-permute-start.32 = (bf16[128,8064]{1,0:T(8,128)(2,1)}, bf16[128,8064]{1,0:T(8,128)(2,1)}, u32[]{:S(2)}, u32[]{:S(2)}) collective-permute-start(bf16[128,8064]{1,0:T(8,128)(2,1)} %pad_maximum_fusion), channel_id=1, source_target_pairs={{0,16},{1,5},{2,18},{3,7},{4,20},{5,9},{6,22},{7,11},{8,24},{9,13}... | collective-permute-start | bytes 6193160 | tf_op jit(solution)/shard_map/ppermute | solution.py:51
  292.1 26.8 %collective-permute-start.33 = (bf16[128,8064]{1,0:T(8,128)(2,1)}, bf16[128,8064]{1,0:T(8,128)(2,1)}, u32[]{:S(2)}, u32[]{:S(2)}) collective-permute-start(bf16[128,8064]{1,0:T(8,128)(2,1)} %pad_maximum_fusion.1), channel_id=1, source_target_pairs={{0,48},{1,13},{2,50},{3,15},{4,52},{5,1},{6,54},{7,3},{8,56},{9,5}... | collective-permute-start | bytes 6193160 | tf_op jit(solution)/shard_map/ppermute | solution.py:51
  311.5 15.8 %collective-permute-start.31 = (bf16[512,4608]{1,0:T(8,128)(2,1)}, bf16[512,4608]{1,0:T(8,128)(2,1)S(1)}, u32[]{:S(2)}, u32[]{:S(2)}) collective-permute-start(bf16[512,4608]{1,0:T(8,128)(2,1)} %get-tuple-element.134), channel_id=1, source_target_pairs={{0,1},{1,0},{2,3},{3,2},{4,5},{5,4},{6,7},{7,6},{8,9},{9,8},{10,11... | collective-permute-start | bytes 14155784 | tf_op jit(solution)/shard_map/ppermute | solution.py:51
  322.9 19.8 %collective-permute-start.34 = (bf16[32,8064]{1,0:T(8,128)(2,1)S(1)}, bf16[32,8064]{1,0:T(8,128)(2,1)S(1)}, u32[]{:S(2)}, u32[]{:S(2)}) collective-permute-start(bf16[32,8064]{1,0:T(8,128)(2,1)S(1)} %get-tuple-element.160), channel_id=1, source_target_pairs={{0,4},{1,17},{2,6},{3,19},{4,8},{5,21},{6,10},{7,23},{8,12},{9,25}... | collective-permute-start | bytes 1548296 | tf_op jit(solution)/shard_map/ppermute | solution.py:51
  323.5 22.7 %collective-permute-start.35 = (bf16[32,8064]{1,0:T(8,128)(2,1)S(1)}, bf16[32,8064]{1,0:T(8,128)(2,1)S(1)}, u32[]{:S(2)}, u32[]{:S(2)}) collective-permute-start(bf16[32,8064]{1,0:T(8,128)(2,1)S(1)} %get-tuple-element.159), channel_id=1, source_target_pairs={{0,8},{1,33},{2,10},{3,35},{4,12},{5,37},{6,14},{7,39},{8,0},{9,41... | collective-permute-start | bytes 1548296 | tf_op jit(solution)/shard_map/ppermute | solution.py:51
  327.3 18.9 %collective-permute-start.36 = (bf16[32,8064]{1,0:T(8,128)(2,1)S(1)}, bf16[32,8064]{1,0:T(8,128)(2,1)S(1)}, u32[]{:S(2)}, u32[]{:S(2)}) collective-permute-start(bf16[32,8064]{1,0:T(8,128)(2,1)S(1)} %get-tuple-element.158), channel_id=1, source_target_pairs={{0,12},{1,49},{2,14},{3,51},{4,0},{5,53},{6,2},{7,55},{8,4},{9,57}... | collective-permute-start | bytes 1548296 | tf_op jit(solution)/shard_map/ppermute | solution.py:51
  327.6 14.8 %collective-permute-start.38 = (bf16[64,4608]{1,0:T(8,128)(2,1)S(1)}, bf16[64,4608]{1,0:T(8,128)(2,1)S(1)}, u32[]{:S(2)}, u32[]{:S(2)}) collective-permute-start(bf16[64,4608]{1,0:T(8,128)(2,1)S(1)} %get-tuple-element.154), channel_id=1, source_target_pairs={{0,48},{1,13},{2,50},{3,15},{4,52},{5,1},{6,54},{7,3},{8,56},{9,5}... | collective-permute-start | bytes 1769480 | tf_op jit(solution)/shard_map/ppermute | solution.py:51
  329.0 13.5 %collective-permute-start.37 = (bf16[64,4608]{1,0:T(8,128)(2,1)S(1)}, bf16[64,4608]{1,0:T(8,128)(2,1)S(1)}, u32[]{:S(2)}, u32[]{:S(2)}) collective-permute-start(bf16[64,4608]{1,0:T(8,128)(2,1)S(1)} %get-tuple-element.155), channel_id=1, source_target_pairs={{0,16},{1,5},{2,18},{3,7},{4,20},{5,9},{6,22},{7,11},{8,24},{9,13}... | collective-permute-start | bytes 1769480 | tf_op jit(solution)/shard_map/ppermute | solution.py:51
  347.6 16.2 %collective-permute-start.39 = (bf16[128,4608]{1,0:T(8,128)(2,1)S(1)}, bf16[128,4608]{1,0:T(8,128)(2,1)S(1)}, u32[]{:S(2)}, u32[]{:S(2)}) collective-permute-start(bf16[128,4608]{1,0:T(8,128)(2,1)S(1)} %pad_maximum_fusion.2), channel_id=1, source_target_pairs={{0,16},{1,5},{2,18},{3,7},{4,20},{5,9},{6,22},{7,11},{8,24},{9,13}... | collective-permute-start | bytes 3538952 | tf_op jit(solution)/shard_map/ppermute | solution.py:51
  349.6 16.2 %collective-permute-start.40 = (bf16[128,4608]{1,0:T(8,128)(2,1)S(1)}, bf16[128,4608]{1,0:T(8,128)(2,1)S(1)}, u32[]{:S(2)}, u32[]{:S(2)}) collective-permute-start(bf16[128,4608]{1,0:T(8,128)(2,1)S(1)} %pad_maximum_fusion.3), channel_id=1, source_target_pairs={{0,48},{1,13},{2,50},{3,15},{4,52},{5,1},{6,54},{7,3},{8,56},{9,5}... | collective-permute-start | bytes 3538952 | tf_op jit(solution)/shard_map/ppermute | solution.py:51
  366.6 11.2 %collective-permute-start.42 = (bf16[32,4608]{1,0:T(8,128)(2,1)S(1)}, bf16[32,4608]{1,0:T(8,128)(2,1)S(1)}, u32[]{:S(2)}, u32[]{:S(2)}) collective-permute-start(bf16[32,4608]{1,0:T(8,128)(2,1)S(1)} %get-tuple-element.164), channel_id=1, source_target_pairs={{0,8},{1,33},{2,10},{3,35},{4,12},{5,37},{6,14},{7,39},{8,0},{9,41... | collective-permute-start | bytes 884744 | tf_op jit(solution)/shard_map/ppermute | solution.py:51
  (35 other events, 289.7 us)
where the time goes:
time: 394 us; the launch traced here: 387 us
  Pallas kernels  151 us (38%)
  waiting for transfers between devices  133 us (34%)
  starting transfers between devices  52.9 us (13%)
  other arithmetic  27 us (7%)
  local copies, waits for them, and re-layouts  18.3 us (5%)
    ppermute x44, waiting for transfers between devices, send(): return lax.ppermute(value, 'fsdp', pairs(kind, step))  112 us
    ppermute x44, starting transfers between devices, send(): return lax.ppermute(value, 'fsdp', pairs(kind, step))  46 us
    pallas_call x2, Pallas kernels, mlp_backward(): pl.pallas_call(functools.partial(mlp_backward_kernel, n, steps), grid=(st...  31 us
    pallas_call x2, Pallas kernels, attn_forward(): pl.pallas_call(functools.partial(attn_forward_kernel, n, row.shape[0], st...  28.2 us
    pallas_call x3, Pallas kernels, product(): pl.pallas_call(functools.partial(product_kernel, counts, len(side_lefts))...  27.8 us
    pallas_call x2, Pallas kernels, mlp_forward(): pl.pallas_call(functools.partial(mlp_forward_kernel, n, steps), grid=(ste...  26.6 us
    pallas_call x2, Pallas kernels, qkv_backward(): pl.pallas_call(functools.partial(qkv_backward_kernel, n, steps), grid=(st...  19.3 us
    pallas_call x2, Pallas kernels, heads_backward(): pl.pallas_call(functools.partial(heads_backward_kernel, n, common[-1].sha...  17.7 us
  transfers between devices with their start and end apart: 46, of which 28 were waited for; matrix products, arithmetic and copies ran while one was open for 7% of the time, Pallas kernels for 13%

commit v1 on v0

--- a/solution.py
+++ b/solution.py
@@ -76,15 +76,15 @@
     return tuple(send(piece, "core") for piece in pieces)
 
 
-def gather(a, m):
+def gather(a, m, order):
     a_z, m = tie(send(a, "z"), m)
-    a, m_z = tie(spread(rows(a, a_z)), send(m, "z"))
+    a, m_z, order = tie(spread(rows(a, a_z)), send(m, "z"), order)
     a_after, a_before = near(a)
     m = spread(rows(m, m_z))
     a_far, a_far2 = far(a_after, a_before)
     a_far, a_far2, m = tie(a_far, a_far2, m)
     a = (a, a_after, a_far, a_far2, a_before)
-    return a + core(*a), (m, *near(m))
+    return a + core(*a), (m, *near(m)), order
 
 
 def add(left, right):
@@ -215,76 +215,64 @@
     return qkv[part, rows, head * HEAD_DIM : (head + 1) * HEAD_DIM]
 
 
-def attn_forward_kernel(n, micro, steps, *refs):
-    u, order, cos, sin, col, row = refs[:6]
-    proj, out, gains = refs[6 : 6 + n], refs[6 + n : 6 + 2 * n], refs[6 + 2 * n : 6 + 3 * n]
-    xn_out, qkv_out, lse_out, o_out, h_out, yn_out, qkv, xn = refs[6 + 3 * n :]
-    step = pl.program_id(0)
-
+def attn_forward_step(step, steps, micro, u, order, cos, sin, col, row, proj, out, gains, xn, qkv, h, yn, saves=None):
     @pl.when(step == 0)
     def _():
         unit, _ = normal(dot(u[...], order[...]))
         xn[...] = (unit * gain_rows(gains)[0:1]).astype(BF)
-        xn_out[...] = xn[...]
 
     packed = dot(xn[...], stack_rows(proj))
 
-    @pl.when(step < steps * 2 // 3)
+    @pl.when(step < 2)
     def _():
         turned = packed * widen(cos[...], ATTN_TILE) + partner(packed) * widen(sin[...], ATTN_TILE)
         qkv[step] = turned.astype(BF)
 
-    @pl.when(step >= steps * 2 // 3)
+    @pl.when(step == 2)
     def _():
         qkv[step] = packed.astype(BF)
-
-    qkv_out[0] = qkv[step]
-
-    @pl.when(step == steps - 1)
-    def _():
         slots = u.shape[0] // micro
         lane = lax.broadcasted_iota(jnp.int32, (slots, 128), 1)
         blocks = []
         for m in range(micro):
-            rows = slice(m * slots, (m + 1) * slots)
-            bias = pair_bias(col[rows], row[m])
+            at = slice(m * slots, (m + 1) * slots)
+            bias = pair_bias(col[at], row[m])
             log_all = jnp.zeros((slots, 128), F32)
             heads = []
             for low in range(0, HEADS, GROUP):
                 group = range(low, low + GROUP)
-                scores = [contract_last(head_of(qkv, 0, k, rows), head_of(qkv, 1, k, rows)) * SCALE + bias for k in group]
+                scores = [contract_last(head_of(qkv, 0, k, at), head_of(qkv, 1, k, at)) * SCALE + bias for k in group]
                 peaks = [jnp.max(x, -1, keepdims=True) for x in scores]
                 scores = [jnp.exp(x - p) for x, p in zip(scores, peaks)]
                 totals = [jnp.sum(x, -1, keepdims=True) for x in scores]
                 for k, p, t in zip(group, peaks, totals):
                     log_all = jnp.where(lane == k, p + jnp.log(t), log_all)
                 probs = [(x * (1.0 / t)).astype(BF) for x, t in zip(scores, totals)]
-                heads += [dot(x, head_of(qkv, 2, k, rows)).astype(BF) for k, x in zip(group, probs)]
-            lse_out[rows] = log_all
+                heads += [dot(x, head_of(qkv, 2, k, at)).astype(BF) for k, x in zip(group, probs)]
+            if saves:
+                saves[0][at] = log_all
             blocks.append(jnp.concatenate(heads, 1))
         attended = dot(jnp.concatenate(blocks, 0), order[...]).astype(BF)
-        o_out[...] = attended
+        if saves:
+            saves[1][...] = attended
         hidden = u[...].astype(F32) + dot(attended, stack_rows(out))
-        h_out[...] = hidden
+        h[...] = hidden
         unit, _ = normal(hidden)
         gain = contract_last(gain_rows(gains).astype(BF), order[...])[1:2]
-        yn_out[...] = dot((unit * gain).astype(BF), order[...]).astype(BF)
-
-
-def mlp_forward_kernel(n, steps, *refs):
-    yn, h, order = refs[:3]
-    gate, up, down = refs[3 : 3 + n], refs[3 + n : 3 + 2 * n], refs[3 + 2 * n : -5]
-    mid_out, one_out, two_out, z_out, total = refs[-5:]
-    step = pl.program_id(0)
+        yn[...] = dot((unit * gain).astype(BF), order[...]).astype(BF)
+
+
+def mlp_forward_step(step, steps, yn, h, order, gate, up, down, z, total, saves=None):
     g = dot(yn[...], stack_rows(gate))
     v = dot(yn[...], stack_rows(up))
     cdf = 0.5 * (1.0 + lax.erf(g * math.sqrt(0.5)))
-    slope = cdf + g * jnp.exp(-0.5 * g * g) * (1.0 / math.sqrt(2.0 * math.pi))
     unit = g * cdf
     mid = (unit * v).astype(BF)
-    mid_out[...] = mid
-    one_out[...] = (v * slope).astype(BF)
-    two_out[...] = unit.astype(BF)
+    if saves:
+        slope = cdf + g * jnp.exp(-0.5 * g * g) * (1.0 / math.sqrt(2.0 * math.pi))
+        at = pl.ds(pl.multiple_of(step * MLP_TILE, 128), MLP_TILE)
+        for ref, value in zip(saves, (mid, (v * slope).astype(BF), unit.astype(BF))):
+            ref[:, at] = value
     part = contract_last(mid, stack_rows(down))
 
     @pl.when(step == 0)
@@ -297,24 +285,20 @@
 
     @pl.when(step == steps - 1)
     def _():
-        z_out[...] = (h[...] + to_absolute(total[...], order[...])).astype(BF)
-
-
-def mlp_backward_kernel(n, steps, *refs):
-    dzr, dz, h, order, one, two = refs[:6]
-    gains, gate, up, down = (refs[6 + k * n : 6 + (k + 1) * n] for k in range(4))
-    dg_out, dv_out, dh_out, da_out, term_out, total = refs[6 + 4 * n :]
-    step = pl.program_id(0)
-
+        z[...] = (h[...] + to_absolute(total[...], order[...])).astype(BF)
+
+
+def mlp_backward_step(step, steps, dzr, dz, h, order, one, two, gains, gate, up, down, dh, da, total, saves=None):
     @pl.when(step == 0)
     def _():
         total[...] = jnp.zeros_like(total)
 
     dmid = dot(dzr[...], stack_rows(down))
-    dg = (dmid * one[...].astype(F32)).astype(BF)
-    dv = (dmid * two[...].astype(F32)).astype(BF)
-    dg_out[...] = dg
-    dv_out[...] = dv
+    dg = (dmid * one.astype(F32)).astype(BF)
+    dv = (dmid * two.astype(F32)).astype(BF)
+    if saves:
+        saves[0][...] = dg
+        saves[1][...] = dv
     total[...] += contract_last(dg, stack_rows(gate)) + contract_last(dv, stack_rows(up))
 
     @pl.when(step == steps - 1)
@@ -322,15 +306,14 @@
         dyn = to_absolute(total[...], order[...])
         unit, scale = normal(h[...])
         gain = contract_last(gain_rows(gains).astype(BF), order[...])[1:2]
-        term_out[...] = dot((dyn * unit).astype(BF), order[...]).astype(BF)
-        dh = dz[...].astype(F32) + normal_back(dyn * gain, unit, scale)
-        dh_out[...] = dh
-        da_out[...] = dh.astype(BF)
-
-
-def heads_backward_kernel(n, micro, *refs):
-    da, order, cos, sin, col, row, qkv, lse = refs[:8]
-    out, dqkv = refs[8 : 8 + n], refs[8 + n]
+        if saves:
+            saves[2][...] = dot((dyn * unit).astype(BF), order[...]).astype(BF)
+        grad = dz[...].astype(F32) + normal_back(dyn * gain, unit, scale)
+        dh[...] = grad
+        da[...] = grad.astype(BF)
+
+
+def heads_backward_step(micro, da, order, cos, sin, col, row, qkv, lse, out, put):
     tokens, width = da.shape
     rel = contract_last(da[...], stack_rows(out)).astype(BF)
     do_all = contract_last(rel, order[...]).astype(BF)
@@ -353,30 +336,105 @@
             dqs += [dot(x, k) for x, k in zip(dss, ks)]
             dks += [contract_first(x, q) for x, q in zip(dss, qs)]
         dq, dk = (jnp.concatenate(x, 1) * SCALE for x in (dqs, dks))
-        dqkv[at, :width] = (dq * cosine - partner(dq) * sine).astype(BF)
-        dqkv[at, width : 2 * width] = (dk * cosine - partner(dk) * sine).astype(BF)
-        dqkv[at, 2 * width :] = jnp.concatenate(dvs, 1).astype(BF)
-
-
-def qkv_backward_kernel(n, steps, *refs):
-    dqkv, dh, u, order = refs[:4]
-    gains, proj = refs[4 : 4 + n], refs[4 + n : 4 + 2 * n]
-    du_out, term_out, total = refs[4 + 2 * n :]
-    step = pl.program_id(0)
-
+        put(0, at, (dq * cosine - partner(dq) * sine).astype(BF))
+        put(1, at, (dk * cosine - partner(dk) * sine).astype(BF))
+        put(2, at, jnp.concatenate(dvs, 1).astype(BF))
+
+
+def qkv_backward_step(step, steps, dqkv, dh, u, order, gains, proj, du, total, term=None):
     @pl.when(step == 0)
     def _():
         total[...] = jnp.zeros_like(total)
 
-    total[...] += contract_last(dqkv[...], stack_rows(proj))
+    total[...] += contract_last(dqkv, stack_rows(proj))
 
     @pl.when(step == steps - 1)
     def _():
         unit, scale = normal(dot(u[...], order[...]))
         dxn = total[...]
-        term_out[...] = (dxn * unit).astype(BF)
+        if term is not None:
+            term[...] = (dxn * unit).astype(BF)
         back = normal_back(dxn * gain_rows(gains)[0:1], unit, scale)
-        du_out[...] = (dh[...] + to_absolute(back, order[...])).astype(BF)
+        du[...] = (dh[...] + to_absolute(back, order[...])).astype(BF)
+
+
+def parted(refs, *sizes):
+    out, low = [], 0
+    for size in sizes:
+        out.append(refs[low : low + size])
+        low += size
+    return *out, refs[low:]
+
+
+def attn_forward_kernel(n, micro, steps, *refs):
+    args, proj, out, gains, rest = parted(refs, 6, n, n, n)
+    h, yn, qkv, xn = rest
+    attn_forward_step(pl.program_id(0), steps, micro, *args, proj, out, gains, xn, qkv, h, yn)
+
+
+def mlp_forward_kernel(n, steps, *refs):
+    args, gate, up, down, rest = parted(refs, 3, n, n, n)
+    mlp_forward_step(pl.program_id(0), steps, *args, gate, up, down, *rest)
+
+
+def mlp_backward_kernel(n, steps, *refs):
+    args, (one, two), gains, gate, up, down, rest = parted(refs, 4, 2, n, n, n, n)
+    dg, dv, dh, da, term, total = rest
+    weights = (gains, gate, up, down)
+    mlp_backward_step(pl.program_id(0), steps, *args, one[...], two[...], *weights, dh, da, total, (dg, dv, term))
+
+
+def heads_backward_kernel(n, micro, *refs):
+    args, out, (dqkv,) = parted(refs, 8, n)
+    width = refs[0].shape[1]
+
+    def put(part, at, value):
+        dqkv[at, part * width : (part + 1) * width] = value
+
+    heads_backward_step(micro, *args, out, put)
+
+
+def middle_kernel(n, micro, *refs):
+    args, proj, out, gains, gate, up, down, outs, scratch = parted(refs, 7, n, n, n, n, n, n, 11)
+    u, dz, order, cos, sin, col, row = args
+    xn, qkv, lse, attended, h, yn, mid, one, two, z, du = outs
+    total, dzr, dh, da, dqkv = scratch
+    step = pl.program_id(0)
+    turns = (cos, sin, col, row)
+
+    @pl.when(step < 3)
+    def _():
+        attn_forward_step(step, 3, micro, u, order, *turns, proj, out, gains, xn, qkv, h, yn, (lse, attended))
+
+    @pl.when((step >= 3) & (step < 6))
+    def _():
+        mlp_forward_step(step - 3, 3, yn, h, order, gate, up, down, z, total, (mid, one, two))
+
+    @pl.when(step == 6)
+    def _():
+        dzr[...] = dot(dz[...], order[...]).astype(BF)
+
+    @pl.when((step >= 6) & (step < 9))
+    def _():
+        at = pl.ds(pl.multiple_of((8 - step) * MLP_TILE, 128), MLP_TILE)
+        weights = (gains, gate, up, down)
+        mlp_backward_step(step - 6, 3, dzr, dz, h, order, one[:, at], two[:, at], *weights, dh, da, total)
+
+    @pl.when(step == 9)
+    def _():
+        def put(part, at, value):
+            dqkv[part, at] = value
+
+        heads_backward_step(micro, da, order, *turns, qkv, lse, out, put)
+
+    @pl.when(step >= 9)
+    def _():
+        qkv_backward_step(step - 9, 3, dqkv[11 - step], dh, u, order, gains, proj, du, total)
+
+
+def qkv_backward_kernel(n, steps, *refs):
+    (dqkv, *args), gains, proj, (du, term, total) = parted(refs, 4, n, n)
+    qkv_backward_step(pl.program_id(0), steps, dqkv[...], *args, gains, proj, du, total, term)
 
 
 def columns(pieces, tile, place):
@@ -406,33 +464,18 @@
 
 
 def attn_forward(u, pieces, common):
-    order, cos, sin, col, row = common
     n, (tokens, width) = len(pieces), u.shape
     steps = 3 * width // ATTN_TILE
     args = (u, *common)
     return pl.pallas_call(
-        functools.partial(attn_forward_kernel, n, row.shape[0], steps),
+        functools.partial(attn_forward_kernel, n, common[-1].shape[0], steps),
         grid=(steps,),
         in_specs=[whole(a) for a in args]
         + columns(pieces, ATTN_TILE, lambda j: j)
         + columns(pieces, width, lambda j: 3)
         + columns(pieces, 128, lambda j: 4 * width // 128),
-        out_specs=[
-            fixed(tokens, width),
-            pl.BlockSpec((1, tokens, ATTN_TILE), lambda j: (j, 0, 0)),
-            fixed(tokens, 128),
-            fixed(tokens, width),
-            fixed(tokens, width),
-            fixed(tokens, width),
-        ],
-        out_shape=[
-            shape_of(tokens, width),
-            jax.ShapeDtypeStruct((steps, tokens, ATTN_TILE), BF),
-            shape_of(tokens, 128, F32),
-            shape_of(tokens, width),
-            shape_of(tokens, width, F32),
-            shape_of(tokens, width),
-        ],
+        out_specs=[fixed(tokens, width), fixed(tokens, width)],
+        out_shape=[shape_of(tokens, width, F32), shape_of(tokens, width)],
         scratch_shapes=[pltpu.VMEM((steps, tokens, ATTN_TILE), BF), pltpu.VMEM((tokens, width), BF)],
         compiler_params=PARAMS,
         cost_estimate=cost(2 * tokens * 6 * width * width, 5 * width * width),
@@ -451,12 +494,50 @@
         + columns(pieces, MLP_TILE, lambda j: j)
         + columns(pieces, MLP_TILE, lambda j: steps + j)
         + columns(pieces, MLP_TILE, lambda j: 2 * steps + j),
-        out_specs=[tiled(tokens, MLP_TILE)] * 3 + [fixed(tokens, width)],
-        out_shape=[shape_of(tokens, hidden)] * 3 + [shape_of(tokens, width)],
+        out_specs=fixed(tokens, width),
+        out_shape=shape_of(tokens, width),
         scratch_shapes=[pltpu.VMEM((tokens, width), F32)],
         compiler_params=PARAMS,
         cost_estimate=cost(6 * tokens * hidden * width, 4 * hidden * width),
     )(*args, *pieces, *pieces, *pieces)
+
+
+def middle(u, dz, common, pieces_a, pieces_m):
+    n, (tokens, width) = len(pieces_a), u.shape
+    hidden = pieces_m[0].shape[1] // 3
+    args = (u, dz, *common)
+
+    def proj_at(j):
+        return jnp.where(j < 3, j, jnp.where(j < 9, 2, 11 - j))
+
+    def mlp_at(j):
+        return jnp.where(j < 6, jnp.maximum(j - 3, 0), jnp.maximum(8 - j, 0))
+
+    kinds = [(width, BF), None, (128, F32), (width, BF), (width, F32), (width, BF)]
+    kinds += [(hidden, BF)] * 3 + [(width, BF)] * 2
+    cube = (3, tokens, width)
+    return pl.pallas_call(
+        functools.partial(middle_kernel, n, common[-1].shape[0]),
+        grid=(12,),
+        in_specs=[whole(a) for a in args]
+        + columns(pieces_a, ATTN_TILE, proj_at)
+        + columns(pieces_a, width, lambda j: 3)
+        + columns(pieces_a, 128, lambda j: 4 * width // 128)
+        + columns(pieces_m, MLP_TILE, mlp_at)
+        + columns(pieces_m, MLP_TILE, lambda j: 3 + mlp_at(j))
+        + columns(pieces_m, MLP_TILE, lambda j: 6 + mlp_at(j)),
+        out_specs=[fixed(tokens, k[0]) if k else pl.BlockSpec(cube, lambda j: (0, 0, 0)) for k in kinds],
+        out_shape=[shape_of(tokens, *k) if k else jax.ShapeDtypeStruct(cube, BF) for k in kinds],
+        scratch_shapes=[
+            pltpu.VMEM((tokens, width), F32),
+            pltpu.VMEM((tokens, width), BF),
+            pltpu.VMEM((tokens, width), F32),
+            pltpu.VMEM((tokens, width), BF),
+            pltpu.VMEM(cube, BF),
+        ],
+        compiler_params=PARAMS,
+        cost_estimate=cost(12 * tokens * (hidden + width) * width, 12 * hidden * width),
+    )(*args, *pieces_a, *pieces_a, *pieces_a, *pieces_m, *pieces_m, *pieces_m)
 
 
 def mlp_backward(dzr, dz, h, one, two, pieces_a, pieces, order):
@@ -579,11 +660,12 @@
     gains = jnp.zeros((gain_attn.shape[1], GAIN_TILE), BF)
     gains = gains.at[:, 0].set(gain_attn[0]).at[:, 1].set(gain_mlp[0])
     gap = jnp.zeros((gain_attn.shape[1], padded - hidden), BF)
-    pieces_a, pieces_m = gather(
+    order = relative_order(lax.axis_index("fsdp"))
+    pieces_a, pieces_m, order = gather(
         jnp.concatenate([attn_proj[0], attn_out[0], gains], 1),
         jnp.concatenate([mlp_in[0, :, :hidden], gap, mlp_in[0, :, hidden:], gap, mlp_out[0], gap], 1),
+        order,
     )
-    order = relative_order(lax.axis_index("fsdp"))
     base = jnp.where(section == 0, 10000.0, 160000.0).astype(F32)
     reach = jnp.where(section == 0, WINDOW / 2.0, 4.0 * slots).astype(F32)
     segment, inner = segment_info(lengths[:, 0], slots)
@@ -596,27 +678,20 @@
     common = (order, jnp.cos(angles), jnp.sin(angles), col, row)
 
     first_in = tokens_in.reshape(tokens, width)
-    _, _, _, _, hid, yn = attn_forward(first_in, pieces_a, common)
+    hid, yn = attn_forward(first_in, pieces_a, common)
     m_block, m_near, m_near2 = pieces_m
     m_near, m_near2, yn = tie(m_near, m_near2, yn)
     m_far, m_far2 = far(m_near, m_near2)
     near_core = core(m_block, m_near, m_near2)
     far_core = core(m_far, m_far2)
     pieces_m = (m_block, m_near, m_far, m_far2, m_near2, *near_core[:2], *far_core, near_core[2])
-    middle_out = mlp_forward(yn, hid, pieces_m, order)[3]
+    middle_out = mlp_forward(yn, hid, pieces_m, order)
     received = lax.ppermute(middle_out, "section", [(0, 1)])
     layer_in = jnp.where(section == 0, first_in, received)
-    xn, qkv, lse, attended, hid, yn = attn_forward(layer_in, pieces_a, common)
-    mid, one, two, result = mlp_forward(yn, hid, pieces_m, order)
-
-    def backward_mlp(grad):
-        rel = dot(grad, order).astype(BF)
-        return mlp_backward(rel, grad, hid, one, two, pieces_a, pieces_m, order)
-
     last_grad = cotangent.reshape(tokens, width)
-    _, _, dh, da, _ = backward_mlp(last_grad)
-    dqkv = heads_backward(da, common, qkv, lse, pieces_a)
-    middle_grad = qkv_backward(dqkv, dh, layer_in, order, pieces_a)[0]
+    xn, qkv, lse, attended, hid, yn, mid, one, two, result, middle_grad = middle(
+        layer_in, last_grad, common, pieces_a, pieces_m
+    )
     received = lax.ppermute(middle_grad, "section", [(1, 0)])
     grad_out = jnp.where(section == 1, last_grad, received)
     half = width // 2
@@ -627,6 +702,7 @@
     got_m = send(sent_m, "core")
     product = make_product((yn, yn, dzr), (dg, dv, mid), MLP_TILE)
     own_m = product(0, cut(half))
+    got_m, da = tie(got_m, da)
     here_m, after_m, far_m, far_m2, before_m = ring_start(own_m, got_m)
     far_m, far_m2 = send(far_m.astype(BF), "first", 1), send(far_m2.astype(BF), "first", -1)
     dqkv = heads_backward(da, common, qkv, lse, pieces_a)

time: 394 us -> 377 us (0.957); the launches traced: 387 us -> 375 us
  waiting for transfers between devices: 133 us -> 123 us
  Pallas kernels: 151 us -> 147 us
    pallas_call x2, Pallas kernels: 28.2 us -> 73 us  [the longest x1 59.7 us: middle(): pl.pallas_call(functools.partial(middle_kernel, n, common[-1].shape[0]),...]
    pallas_call x2 -> x1, Pallas kernels: 31 us -> 15.3 us  [mlp_backward(): pl.pallas_call(functools.partial(mlp_backward_kernel, n, steps), grid=(st...]
    pallas_call x2 -> x1, Pallas kernels: 26.6 us -> 12.2 us  [mlp_forward(): pl.pallas_call(functools.partial(mlp_forward_kernel, n, steps), grid=(ste...]
    ppermute x44, waiting for transfers between devices: 112 us -> 101 us  [send(): return lax.ppermute(value, 'fsdp', pairs(kind, step))]
    pallas_call x2 -> x1, Pallas kernels: 19.3 us -> 9.62 us  [qkv_backward(): pl.pallas_call(functools.partial(qkv_backward_kernel, n, steps), grid=(st...]
    pallas_call x2 -> x1, Pallas kernels: 17.7 us -> 8.78 us  [heads_backward(): pl.pallas_call(functools.partial(heads_backward_kernel, n, common[-1].sha...]
  transfers between devices with their start and end apart: 46 -> 46, of which waited for: 28 -> 29; matrix products, arithmetic and copies ran while one was open for 7% -> 7% of each run, Pallas kernels for 13% -> 13%
where the time goes in v1:
time: 377 us; the launch traced here: 375 us
  Pallas kernels  147 us (39%)
  waiting for transfers between devices  123 us (33%)
  starting transfers between devices  53.9 us (14%)
  other arithmetic  27.9 us (7%)
  local copies, waits for them, and re-layouts  20.5 us (5%)
    ppermute x44, waiting for transfers between devices, send(): return lax.ppermute(value, 'fsdp', pairs(kind, step))  101 us
    pallas_call x1, Pallas kernels, middle(): pl.pallas_call(functools.partial(middle_kernel, n, common[-1].shape[0]),...  59.7 us
    ppermute x44, starting transfers between devices, send(): return lax.ppermute(value, 'fsdp', pairs(kind, step))  47 us
    pallas_call x3, Pallas kernels, product(): pl.pallas_call(functools.partial(product_kernel, counts, len(side_lefts))...  27.8 us
    pallas_call x1, Pallas kernels, mlp_backward(): pl.pallas_call(functools.partial(mlp_backward_kernel, n, steps), grid=(st...  15.3 us
    pallas_call x1, Pallas kernels, attn_forward(): pl.pallas_call(functools.partial(attn_forward_kernel, n, common[-1].shape...  13.3 us
    ppermute x1, waiting for transfers between devices, shards(): received = lax.ppermute(middle_grad, 'section', [(1, 0)])  12.6 us
    pallas_call x1, Pallas kernels, mlp_forward(): pl.pallas_call(functools.partial(mlp_forward_kernel, n, steps), grid=(ste...  12.2 us
  transfers between devices with their start and end apart: 46, of which 29 were waited for; matrix products, arithmetic and copies ran while one was open for 7% of the time, Pallas kernels for 13%

profile of v1, /device:TPU:8, one launch (start us, length us, event | category | flops | bytes accessed | tf_op | source)
XLA Modules:
  0.0 374.8 jit_solution(8151358317920176171)
XLA Ops:
  12.0 2.8 collective-permute-start.1
  31.4 10.0 %collective-permute-done.9 = bf16[32,8064]{1,0:T(8,128)(2,1)S(1)} collective-permute-done((bf16[32,8064]{1,0:T(8,128)(2,1)S(1)}, bf16[32,8064]{1,0:T(8,128)(2,1)S(1)}, u32[]{:S(2)}, u32[]{:S(2)}) %collective-permute-start.9) | collective-permute-done | bytes 516128 | tf_op jit(solution)/shard_map/ppermute | solution.py:51
  45.2 4.8 %collective-permute-done.5.refs_7_.refs_17_.refs_27_.refs_8_.refs_18_.refs_28_.refs_9_.refs_5_.refs_15_ = bf16[128,4224]{1,0:T(8,128)(2,1)S(1)} collective-permute-done((bf16[128,4224]{1,0:T(8,128)(2,1)}, bf16[128,4224]{1,0:T(8,128)(2,1)S(1)}, u32[]{:S(2)}, u32[]{:S(2)}) %collective-permute-start.5) | collective-permute-done | bytes 1081376 | tf_op jit(solution)/shard_map/ppermute | solution.py:51
  53.3 6.2 %collective-permute-done.6.refs_8_.refs_18_.refs_28_.refs_9_.refs_19_.refs_29_.refs_10_.refs_6_.refs_16_ = bf16[64,4224]{1,0:T(8,128)(2,1)} collective-permute-done((bf16[64,4224]{1,0:T(8,128)(2,1)S(1)}, bf16[64,4224]{1,0:T(8,128)(2,1)}, u32[]{:S(2)}, u32[]{:S(2)}) %collective-permute-start.6) | collective-permute-done | bytes 540704 | tf_op jit(solution)/shard_map/ppermute | solution.py:51
  59.5 3.0 collective-permute-done.8.refs_9_.refs_19_.refs_29_.refs_10_.refs_20_.refs_30_.refs_11_.refs_7_.refs_17_
  62.5 3.2 collective-permute-start.12
  73.5 13.3 %shard_map.152 = (f32[192,1024]{1,0:T(8,128)}, bf16[192,1024]{1,0:T(8,128)(2,1)}) custom-call(bf16[192,1024]{1,0:T(8,128)(2,1)} %bitcast.41, bf16[1024,1024]{1,0:T(8,128)(2,1)} %fusion.refs_1_.refs_2_.refs_3_, f32[192,128]{1,0:T(8,128)} %copy.47.refs_2_.refs_3_, f32[192,128]{1,0:T(8,128)} %copy.48.refs_3_.refs_4_, ...), custom_call_target="tpu_custom_call" | custom-call | flops 37748736 | bytes 163840 | tf_op jit(solution)/shard_map/pallas_call | solution.py:470
  95.8 10.7 %collective-permute-done.19.refs_5_.refs_15_.refs_25_.refs_39_.refs_49_.refs_59_.refs_18_.refs_28_.refs_38_ = bf16[64,8064]{1,0:T(8,128)(2,1)S(1)} collective-permute-done((bf16[64,8064]{1,0:T(8,128)(2,1)S(1)}, bf16[64,8064]{1,0:T(8,128)(2,1)S(1)}, u32[]{:S(2)}, u32[]{:S(2)}) %collective-permute-start.19) | collective-permute-done | bytes 1032224 | tf_op jit(solution)/shard_map/ppermute | solution.py:51
  113.4 12.2 %shard_map.153 = bf16[192,1024]{1,0:T(8,128)(2,1)} custom-call(bf16[192,1024]{1,0:T(8,128)(2,1)} %get-tuple-element.99.refs_0_, f32[192,1024]{1,0:T(8,128)} %get-tuple-element.100.refs_1_, bf16[1024,1024]{1,0:T(8,128)(2,1)} %fusion.refs_1_.refs_2_.refs_3_, ...), custom_call_target="tpu_custom_call" | custom-call | flops 49545216 | bytes 344064 | tf_op jit(solution)/shard_map/pallas_call | solution.py:490
  125.6 5.5 %collective-permute-start.26 = (bf16[192,1024]{1,0:T(8,128)(2,1)}, bf16[192,1024]{1,0:T(8,128)(2,1)S(1)}, u32[]{:S(2)}, u32[]{:S(2)}) collective-permute-start(bf16[192,1024]{1,0:T(8,128)(2,1)} %shard_map.153), channel_id=1, source_target_pairs={{0,64},{1,65},{2,66},{3,67},{4,68},{5,69},{6,70},{7,71},{8,72},{9,... | collective-permute-start | bytes 1179656 | tf_op jit(solution)/shard_map/ppermute | solution.py:689
  131.1 8.9 %collective-permute-done.26 = bf16[192,1024]{1,0:T(8,128)(2,1)S(1)} collective-permute-done((bf16[192,1024]{1,0:T(8,128)(2,1)}, bf16[192,1024]{1,0:T(8,128)(2,1)S(1)}, u32[]{:S(2)}, u32[]{:S(2)}) %collective-permute-start.26) | collective-permute-done | bytes 393248 | tf_op jit(solution)/shard_map/ppermute | solution.py:689
  140.9 59.7 %shard_map.154 = (bf16[192,1024]{1,0:T(8,128)(2,1)}, bf16[3,192,1024]{2,1,0:T(8,128)(2,1)}, f32[192,128]{1,0:T(8,128)}, bf16[192,1024]{1,0:T(8,128)(2,1)}, f32[1...) custom-call(bf16[192,1024]{1,0:T(8,128)(2,1)} %broadcast_select_fusi, ...), custom_call_target="tpu_custom_call" | custom-call | flops 136839168 | bytes 1032192 | tf_op jit(solution)/shard_map/pallas_call | solution.py:519
  201.9 12.6 %collective-permute-done.27 = bf16[192,1024]{1,0:T(8,128)(2,1)S(1)} collective-permute-done((bf16[192,1024]{1,0:T(8,128)(2,1)}, bf16[192,1024]{1,0:T(8,128)(2,1)S(1)}, u32[]{:S(2)}, u32[]{:S(2)}) %collective-permute-start.27) | collective-permute-done | bytes 393248 | tf_op jit(solution)/shard_map/ppermute | solution.py:695
  216.0 15.3 %shard_map.155 = (bf16[192,2688]{1,0:T(8,128)(2,1)}, bf16[192,2688]{1,0:T(8,128)(2,1)}, f32[192,1024]{1,0:T(8,128)}, bf16[192,1024]{1,0:T(8,128)(2,1)}, bf16[192,1024]{1,0:T(8,128)(2,1)}) custom-call(bf16[192,1024]{1,0:T(8,128)(2,1)} %convolution_convert_fusion.refs_0_.refs_2_, bf16[192,1024]{1,0:T(8,128)(2,1)} %copy-done.12, ...), custom_call_target="tpu_custom_call" | custom-call | flops 49545216 | bytes 344064 | tf_op jit(solution)/shard_map/pallas_call | solution.py:548
  231.3 9.7 %shard_map.156 = bf16[512,8064]{1,0:T(8,128)(2,1)} custom-call(bf16[192,1024]{1,0:T(8,128)(2,1)} %get-tuple-element.112.refs_0_.refs_1_, bf16[192,1024]{1,0:T(8,128)(2,1)} %get-tuple-element.112.refs_0_.refs_1_, bf16[192,1024]{1,0:T(8,128)(2,1)} %convolution_convert_fusion.refs_0_.refs_2_, bf16[192,2688]{1,0:T(8,128)(2,1)} %get-tuple-element.109.refs_3_, ...), custom_call_target="tpu_custom_call" | custom-call | flops 24772608 | bytes 129024 | tf_op jit(solution)/shard_map/pallas_call | solution.py:638
  241.1 9.8 %shard_map.157 = (bf16[128,8064]{1,0:T(8,128)(2,1)}, bf16[128,8064]{1,0:T(8,128)(2,1)}, bf16[64,8064]{1,0:T(8,128)(2,1)}, bf16[64,8064]{1,0:T(8,128)(2,1)}, bf16[128,8064]{1,0:T(8,128)(2,1)}) custom-call(bf16[192,1024]{1,0:T(8,128)(2,1)} %get-tuple-element.112.refs_0_.refs_1_, bf16[192,1024]{1,0:T(8,128)(2,1)} %get-tuple-element.112.refs_0_.refs_1_, ...), custom_call_target="tpu_custom_call" | custom-call | flops 24772608 | bytes 129024 | tf_op jit(solution)/shard_map/pallas_call | solution.py:638
  250.9 3.5 collective-permute-done.28
  254.4 4.1 %add_convert_fusion.2 = (bf16[64,8064]{1,0:T(8,128)(2,1)}, bf16[64,8064]{1,0:T(8,128)(2,1)}) fusion(bf16[64,8064]{1,0:T(8,128)(2,1)} %get-tuple-element.118, bf16[512,8064]{1,0:T(8,128)(2,1)} %collective-permute-done.28, bf16[64,8064]{1,0:T(8,128)(2,1)} %get-tuple-element.117), kind=kLoop, calls=%fused_computation.16 | loop fusion | flops 4128768 | bytes 6193152 | tf_op jit(solution)/shard_map/convert_element_type | solution.py:707
  260.6 3.1 convert_add_fusion
  265.9 8.8 %shard_map.158.refs_0_.refs_4_ = bf16[192,3072]{1,0:T(8,128)(2,1)} custom-call(bf16[192,1024]{1,0:T(8,128)(2,1)} %get-tuple-element.119.refs_0_.refs_5_, bf16[1024,1024]{1,0:T(8,128)(2,1)} %fusion.refs_1_.refs_2_.refs_3_, f32[192,128]{1,0:T(8,128)} %copy.47.refs_2_.refs_3_, f32[192,128]{1,0:T(8,128)} %copy.48.refs_3_.refs_4_, ...), custom_call_target="tpu_custom_call" | custom-call | flops 6291456 | bytes 32768 | tf_op jit(solution)/shard_map/pallas_call | solution.py:569
  281.8 9.6 %shard_map.159 = (bf16[192,1024]{1,0:T(8,128)(2,1)}, bf16[192,1024]{1,0:T(8,128)(2,1)}) custom-call(bf16[192,3072]{1,0:T(8,128)(2,1)} %shard_map.158.refs_0_.refs_4_, f32[192,1024]{1,0:T(8,128)} %get-tuple-element.127.refs_1_, bf16[192,1024]{1,0:T(8,128)(2,1)} %broadcast_select_fusion.1.refs_0_.refs_2_, bf16[1024,1024]{1,0:T(8,128)(2,1)} %fusion.refs_1_.refs_2_.refs_3_, ...), custom_call_target="tpu_custom_call" | custom-call | flops 18874368 | bytes 98304 | tf_op jit(solution)/shard_map/pallas_call | solution.py:584
  292.8 8.3 %shard_map.160 = (bf16[128,4608]{1,0:T(8,128)(2,1)}, bf16[128,4608]{1,0:T(8,128)(2,1)}, bf16[64,4608]{1,0:T(8,128)(2,1)}, bf16[64,4608]{1,0:T(8,128)(2,1)}, bf16...) custom-call(bf16[192,1024]{1,0:T(8,128)(2,1)} %get-tuple-element.129.refs_0_, ...), custom_call_target="tpu_custom_call" | custom-call | flops 28311552 | bytes 147456 | tf_op jit(solution)/shard_map/pallas_call | solution.py:638
  301.1 3.0 collective-permute-start.31
  306.9 2.6 add_convert_fusion
  311.3 4.5 %collective-permute-start.35 = (bf16[32,8064]{1,0:T(8,128)(2,1)S(1)}, bf16[32,8064]{1,0:T(8,128)(2,1)S(1)}, u32[]{:S(2)}, u32[]{:S(2)}) collective-permute-start(bf16[32,8064]{1,0:T(8,128)(2,1)S(1)} %get-tuple-element.159), channel_id=1, source_target_pairs={{0,8},{1,33},{2,10},{3,35},{4,12},{5,37},{6,14},{7,39},{8,0},{9,41... | collective-permute-start | bytes 1548296 | tf_op jit(solution)/shard_map/ppermute | solution.py:51
  319.2 13.4 %collective-permute-done.38 = bf16[64,4608]{1,0:T(8,128)(2,1)S(1)} collective-permute-done((bf16[64,4608]{1,0:T(8,128)(2,1)S(1)}, bf16[64,4608]{1,0:T(8,128)(2,1)S(1)}, u32[]{:S(2)}, u32[]{:S(2)}) %collective-permute-start.38) | collective-permute-done | bytes 589856 | tf_op jit(solution)/shard_map/ppermute | solution.py:51
  338.1 4.7 %collective-permute-done.45 = bf16[16,8064]{1,0:T(8,128)(2,1)S(1)} collective-permute-done((bf16[16,8064]{1,0:T(8,128)(2,1)S(1)}, bf16[16,8064]{1,0:T(8,128)(2,1)S(1)}, u32[]{:S(2)}, u32[]{:S(2)}) %collective-permute-start.45) | collective-permute-done | bytes 258080 | tf_op jit(solution)/shard_map/ppermute | solution.py:51
  342.8 9.5 %collective-permute-done.39 = bf16[128,4608]{1,0:T(8,128)(2,1)S(1)} collective-permute-done((bf16[128,4608]{1,0:T(8,128)(2,1)S(1)}, bf16[128,4608]{1,0:T(8,128)(2,1)S(1)}, u32[]{:S(2)}, u32[]{:S(2)}) %collective-permute-start.39) | collective-permute-done | bytes 1179680 | tf_op jit(solution)/shard_map/ppermute | solution.py:51
  355.1 3.3 collective-permute-start.42
  359.2 3.9 %collective-permute-done.41 = bf16[32,4608]{1,0:T(8,128)(2,1)S(1)} collective-permute-done((bf16[32,4608]{1,0:T(8,128)(2,1)S(1)}, bf16[32,4608]{1,0:T(8,128)(2,1)S(1)}, u32[]{:S(2)}, u32[]{:S(2)}) %collective-permute-start.41) | collective-permute-done | bytes 294944 | tf_op jit(solution)/shard_map/ppermute | solution.py:51
  363.0 3.3 collective-permute-done.42
  369.3 3.2 collective-permute-done.44
  (209 shorter events, 96.8 us)
Async XLA Ops:
  15.6 10.1 %collective-permute-start.3 = (bf16[32,4224]{1,0:T(8,128)(2,1)S(1)}, bf16[32,4224]{1,0:T(8,128)(2,1)S(1)}, u32[]{:S(2)}, u32[]{:S(2)}) collective-permute-start(bf16[32,4224]{1,0:T(8,128)(2,1)S(1)} %pad_maximum_fusion.4), channel_id=1, source_target_pairs={{0,4},{1,17},{2,6},{3,19},{4,8},{5,21},{6,10},{7,23},{8,12},{9,25}... | collective-permute-start | bytes 811016 | tf_op jit(solution)/shard_map/ppermute | solution.py:51
  16.5 9.9 %collective-permute-start.4 = (bf16[16,8064]{1,0:T(8,128)(2,1)S(1)}, bf16[16,8064]{1,0:T(8,128)(2,1)S(1)}, u32[]{:S(2)}, u32[]{:S(2)}) collective-permute-start(bf16[16,8064]{1,0:T(8,128)(2,1)S(1)} %concatenate.50), channel_id=1, source_target_pairs={{0,2},{1,3},{2,0},{3,1},{4,6},{5,7},{6,4},{7,5},{8,10},{9,11},{10,... | collective-permute-start | bytes 774152 | tf_op jit(solution)/shard_map/ppermute | solution.py:51
  27.2 14.3 %collective-permute-start.9 = (bf16[32,8064]{1,0:T(8,128)(2,1)S(1)}, bf16[32,8064]{1,0:T(8,128)(2,1)S(1)}, u32[]{:S(2)}, u32[]{:S(2)}) collective-permute-start(bf16[32,8064]{1,0:T(8,128)(2,1)S(1)} %get-tuple-element.172), channel_id=1, source_target_pairs={{0,12},{1,49},{2,14},{3,51},{4,0},{5,53},{6,2},{7,55},{8,4},{9,57}... | collective-permute-start | bytes 1548296 | tf_op jit(solution)/shard_map/ppermute | solution.py:51
  28.3 16.0 %collective-permute-start.10 = (bf16[32,8064]{1,0:T(8,128)(2,1)S(1)}, bf16[32,8064]{1,0:T(8,128)(2,1)S(1)}, u32[]{:S(2)}, u32[]{:S(2)}) collective-permute-start(bf16[32,8064]{1,0:T(8,128)(2,1)S(1)} %get-tuple-element.172), channel_id=1, source_target_pairs={{0,8},{1,33},{2,10},{3,35},{4,12},{5,37},{6,14},{7,39},{8,0},{9,41... | collective-permute-start | bytes 1548296 | tf_op jit(solution)/shard_map/ppermute | solution.py:51
  28.5 23.9 %collective-permute-start.11 = (bf16[32,8064]{1,0:T(8,128)(2,1)S(1)}, bf16[32,8064]{1,0:T(8,128)(2,1)S(1)}, u32[]{:S(2)}, u32[]{:S(2)}) collective-permute-start(bf16[32,8064]{1,0:T(8,128)(2,1)S(1)} %get-tuple-element.172), channel_id=1, source_target_pairs={{0,4},{1,17},{2,6},{3,19},{4,8},{5,21},{6,10},{7,23},{8,12},{9,25}... | collective-permute-start | bytes 1548296 | tf_op jit(solution)/shard_map/ppermute | solution.py:51
  29.4 20.6 %collective-permute-start.5 = (bf16[128,4224]{1,0:T(8,128)(2,1)}, bf16[128,4224]{1,0:T(8,128)(2,1)S(1)}, u32[]{:S(2)}, u32[]{:S(2)}) collective-permute-start(bf16[128,4224]{1,0:T(8,128)(2,1)} %constant_dynamic-update-slice_fusion.refs_6_.refs_16_.refs_26_.refs_7_.refs_17_.refs_27_.refs_8_.refs_4_.refs_14_), channel_id=1, source_target_pairs={{0,48},{1,13},{2,50},{3,15},{4,52},{5,1},{6,54},{7,3},{8,56},{9,5}... | collective-permute-start | bytes 3244040 | tf_op jit(solution)/shard_map/ppermute | solution.py:51
  29.8 21.7 %collective-permute-start.7 = (bf16[128,4224]{1,0:T(8,128)(2,1)}, bf16[128,4224]{1,0:T(8,128)(2,1)S(1)}, u32[]{:S(2)}, u32[]{:S(2)}) collective-permute-start(bf16[128,4224]{1,0:T(8,128)(2,1)} %constant_dynamic-update-slice_fusion.refs_6_.refs_16_.refs_26_.refs_7_.refs_17_.refs_27_.refs_8_.refs_4_.refs_14_), channel_id=1, source_target_pairs={{0,16},{1,5},{2,18},{3,7},{4,20},{5,9},{6,22},{7,11},{8,24},{9,13}... | collective-permute-start | bytes 3244040 | tf_op jit(solution)/shard_map/ppermute | solution.py:51
  41.4 25.9 %collective-permute-start.14 = (bf16[128,4224]{1,0:T(8,128)(2,1)}, bf16[128,4224]{1,0:T(8,128)(2,1)}, u32[]{:S(2)}, u32[]{:S(2)}) collective-permute-start(bf16[128,4224]{1,0:T(8,128)(2,1)} %constant_dynamic-update-slice_fusion.refs_6_.refs_16_.refs_26_.refs_7_.refs_17_.refs_27_.refs_8_.refs_4_.refs_14_), channel_id=1, source_target_pairs={{0,1},{1,0},{2,3},{3,2},{4,5},{5,4},{6,7},{7,6},{8,9},{9,8},{10,11... | collective-permute-start | bytes 3244040 | tf_op jit(solution)/shard_map/ppermute | solution.py:51
  51.6 10.9 %collective-permute-start.8 = (bf16[64,4224]{1,0:T(8,128)(2,1)S(1)}, bf16[64,4224]{1,0:T(8,128)(2,1)}, u32[]{:S(2)}, u32[]{:S(2)}) collective-permute-start(bf16[64,4224]{1,0:T(8,128)(2,1)S(1)} %slice.214), channel_id=1, source_target_pairs={{0,16},{1,5},{2,18},{3,7},{4,20},{5,9},{6,22},{7,11},{8,24},{9,13}... | collective-permute-start | bytes 1622024 | tf_op jit(solution)/shard_map/ppermute | solution.py:51
  62.5 26.7 %collective-permute-start.12 = (bf16[128,8064]{1,0:T(8,128)(2,1)}, bf16[128,8064]{1,0:T(8,128)(2,1)S(1)}, u32[]{:S(2)}, u32[]{:S(2)}) collective-permute-start(bf16[128,8064]{1,0:T(8,128)(2,1)} %constant_dynamic-update-slice_fusion.7.refs_3_.refs_13_.refs_23_.refs_37_.refs_47_.refs_57_.refs_16_.refs_26_.refs_36_), channel_id=1, source_target_pairs={{0,48},{1,13},{2,50},{3,15},{4,52},{5,1},{6,54},{7,3},{8,56},{9,5}... | collective-permute-start | bytes 6193160 | tf_op jit(solution)/shard_map/ppermute | solution.py:51
  65.7 26.0 %collective-permute-start.13 = (bf16[128,8064]{1,0:T(8,128)(2,1)}, bf16[128,8064]{1,0:T(8,128)(2,1)}, u32[]{:S(2)}, u32[]{:S(2)}) collective-permute-start(bf16[128,8064]{1,0:T(8,128)(2,1)} %constant_dynamic-update-slice_fusion.7.refs_3_.refs_13_.refs_23_.refs_37_.refs_47_.refs_57_.refs_16_.refs_26_.refs_36_), channel_id=1, source_target_pairs={{0,16},{1,5},{2,18},{3,7},{4,20},{5,9},{6,22},{7,11},{8,24},{9,13}... | collective-permute-start | bytes 6193160 | tf_op jit(solution)/shard_map/ppermute | solution.py:51
  73.0 36.1 %collective-permute-start.21 = (bf16[128,8064]{1,0:T(8,128)(2,1)}, bf16[128,8064]{1,0:T(8,128)(2,1)S(1)}, u32[]{:S(2)}, u32[]{:S(2)}) collective-permute-start(bf16[128,8064]{1,0:T(8,128)(2,1)} %constant_dynamic-update-slice_fusion.7.refs_3_.refs_13_.refs_23_.refs_37_.refs_47_.refs_57_.refs_16_.refs_26_.refs_36_), channel_id=1, source_target_pairs={{0,1},{1,0},{2,3},{3,2},{4,5},{5,4},{6,7},{7,6},{8,9},{9,8},{10,11... | collective-permute-start | bytes 6193160 | tf_op jit(solution)/shard_map/ppermute | solution.py:51
  91.8 14.7 %collective-permute-start.19 = (bf16[64,8064]{1,0:T(8,128)(2,1)S(1)}, bf16[64,8064]{1,0:T(8,128)(2,1)S(1)}, u32[]{:S(2)}, u32[]{:S(2)}) collective-permute-start(bf16[64,8064]{1,0:T(8,128)(2,1)S(1)} %slice.172), channel_id=1, source_target_pairs={{0,48},{1,13},{2,50},{3,15},{4,52},{5,1},{6,54},{7,3},{8,56},{9,5}... | collective-permute-start | bytes 3096584 | tf_op jit(solution)/shard_map/ppermute | solution.py:51
  94.4 14.7 %collective-permute-start.20 = (bf16[64,8064]{1,0:T(8,128)(2,1)S(1)}, bf16[64,8064]{1,0:T(8,128)(2,1)S(1)}, u32[]{:S(2)}, u32[]{:S(2)}) collective-permute-start(bf16[64,8064]{1,0:T(8,128)(2,1)S(1)} %slice.173), channel_id=1, source_target_pairs={{0,16},{1,5},{2,18},{3,7},{4,20},{5,9},{6,22},{7,11},{8,24},{9,13}... | collective-permute-start | bytes 3096584 | tf_op jit(solution)/shard_map/ppermute | solution.py:51
  95.3 16.5 %collective-permute-start.22 = (bf16[128,8064]{1,0:T(8,128)(2,1)S(1)}, bf16[128,8064]{1,0:T(8,128)(2,1)S(1)}, u32[]{:S(2)}, u32[]{:S(2)}) collective-permute-start(bf16[128,8064]{1,0:T(8,128)(2,1)S(1)} %collective-permute-done.12.refs_4_.refs_14_.refs_24_.refs_38_.refs_48_.refs_58_.refs_17_.refs_27_.refs_37_), channel_id=1, source_target_pairs={{0,1},{1,0},{2,3},{3,2},{4,5},{5,4},{6,7},{7,6},{8,9},{9,8},{10,11... | collective-permute-start | bytes 6193160 | tf_op jit(solution)/shard_map/ppermute | solution.py:51
  95.3 16.5 %collective-permute-start.25 = (bf16[128,8064]{1,0:T(8,128)(2,1)}, bf16[128,8064]{1,0:T(8,128)(2,1)}, u32[]{:S(2)}, u32[]{:S(2)}) collective-permute-start(bf16[128,8064]{1,0:T(8,128)(2,1)} %collective-permute-done.13.refs_7_.refs_17_.refs_27_.refs_41_.refs_51_.refs_61_.refs_20_.refs_30_.refs_40_), channel_id=1, source_target_pairs={{0,1},{1,0},{2,3},{3,2},{4,5},{5,4},{6,7},{7,6},{8,9},{9,8},{10,11... | collective-permute-start | bytes 6193160 | tf_op jit(solution)/shard_map/ppermute | solution.py:51
  125.6 14.5 %collective-permute-start.26 = (bf16[192,1024]{1,0:T(8,128)(2,1)}, bf16[192,1024]{1,0:T(8,128)(2,1)S(1)}, u32[]{:S(2)}, u32[]{:S(2)}) collective-permute-start(bf16[192,1024]{1,0:T(8,128)(2,1)} %shard_map.153), channel_id=1, source_target_pairs={{0,64},{1,65},{2,66},{3,67},{4,68},{5,69},{6,70},{7,71},{8,72},{9,... | collective-permute-start | bytes 1179656 | tf_op jit(solution)/shard_map/ppermute | solution.py:689
  200.6 13.9 %collective-permute-start.27 = (bf16[192,1024]{1,0:T(8,128)(2,1)}, bf16[192,1024]{1,0:T(8,128)(2,1)S(1)}, u32[]{:S(2)}, u32[]{:S(2)}) collective-permute-start(bf16[192,1024]{1,0:T(8,128)(2,1)} %get-tuple-element.105), channel_id=1, source_target_pairs={{64,0},{65,1},{66,2},{67,3},{68,4},{69,5},{70,6},{71,7},{72,8},{73... | collective-permute-start | bytes 1179656 | tf_op jit(solution)/shard_map/ppermute | solution.py:695
  241.1 13.3 %collective-permute-start.28 = (bf16[512,8064]{1,0:T(8,128)(2,1)}, bf16[512,8064]{1,0:T(8,128)(2,1)}, u32[]{:S(2)}, u32[]{:S(2)}) collective-permute-start(bf16[512,8064]{1,0:T(8,128)(2,1)} %shard_map.156), channel_id=1, source_target_pairs={{0,1},{1,0},{2,3},{3,2},{4,5},{5,4},{6,7},{7,6},{8,9},{9,8},{10,11... | collective-permute-start | bytes 24772616 | tf_op jit(solution)/shard_map/ppermute | solution.py:51
  258.5 16.2 %collective-permute-start.29 = (bf16[64,8064]{1,0:T(8,128)(2,1)}, bf16[64,8064]{1,0:T(8,128)(2,1)}, u32[]{:S(2)}, u32[]{:S(2)}) collective-permute-start(bf16[64,8064]{1,0:T(8,128)(2,1)} %get-tuple-element.153), channel_id=1, source_target_pairs={{0,16},{1,5},{2,18},{3,7},{4,20},{5,9},{6,22},{7,11},{8,24},{9,13}... | collective-permute-start | bytes 3096584 | tf_op jit(solution)/shard_map/ppermute | solution.py:51
  259.3 15.4 %collective-permute-start.30 = (bf16[64,8064]{1,0:T(8,128)(2,1)}, bf16[64,8064]{1,0:T(8,128)(2,1)}, u32[]{:S(2)}, u32[]{:S(2)}) collective-permute-start(bf16[64,8064]{1,0:T(8,128)(2,1)} %get-tuple-element.152), channel_id=1, source_target_pairs={{0,48},{1,13},{2,50},{3,15},{4,52},{5,1},{6,54},{7,3},{8,56},{9,5}... | collective-permute-start | bytes 3096584 | tf_op jit(solution)/shard_map/ppermute | solution.py:51
  279.3 26.3 %collective-permute-start.32 = (bf16[128,8064]{1,0:T(8,128)(2,1)}, bf16[128,8064]{1,0:T(8,128)(2,1)S(1)}, u32[]{:S(2)}, u32[]{:S(2)}) collective-permute-start(bf16[128,8064]{1,0:T(8,128)(2,1)} %pad_maximum_fusion), channel_id=1, source_target_pairs={{0,16},{1,5},{2,18},{3,7},{4,20},{5,9},{6,22},{7,11},{8,24},{9,13}... | collective-permute-start | bytes 6193160 | tf_op jit(solution)/shard_map/ppermute | solution.py:51
  280.2 26.7 %collective-permute-start.33 = (bf16[128,8064]{1,0:T(8,128)(2,1)S(1)}, bf16[128,8064]{1,0:T(8,128)(2,1)S(1)}, u32[]{:S(2)}, u32[]{:S(2)}) collective-permute-start(bf16[128,8064]{1,0:T(8,128)(2,1)S(1)} %pad_maximum_fusion.1), channel_id=1, source_target_pairs={{0,48},{1,13},{2,50},{3,15},{4,52},{5,1},{6,54},{7,3},{8,56},{9,5}... | collective-permute-start | bytes 6193160 | tf_op jit(solution)/shard_map/ppermute | solution.py:51
  301.1 14.7 %collective-permute-start.31 = (bf16[512,4608]{1,0:T(8,128)(2,1)}, bf16[512,4608]{1,0:T(8,128)(2,1)S(1)}, u32[]{:S(2)}, u32[]{:S(2)}) collective-permute-start(bf16[512,4608]{1,0:T(8,128)(2,1)} %get-tuple-element.134), channel_id=1, source_target_pairs={{0,1},{1,0},{2,3},{3,2},{4,5},{5,4},{6,7},{7,6},{8,9},{9,8},{10,11... | collective-permute-start | bytes 14155784 | tf_op jit(solution)/shard_map/ppermute | solution.py:51
  309.6 23.3 %collective-permute-start.34 = (bf16[32,8064]{1,0:T(8,128)(2,1)S(1)}, bf16[32,8064]{1,0:T(8,128)(2,1)S(1)}, u32[]{:S(2)}, u32[]{:S(2)}) collective-permute-start(bf16[32,8064]{1,0:T(8,128)(2,1)S(1)} %get-tuple-element.160), channel_id=1, source_target_pairs={{0,4},{1,17},{2,6},{3,19},{4,8},{5,21},{6,10},{7,23},{8,12},{9,25}... | collective-permute-start | bytes 1548296 | tf_op jit(solution)/shard_map/ppermute | solution.py:51
  311.3 23.4 %collective-permute-start.35 = (bf16[32,8064]{1,0:T(8,128)(2,1)S(1)}, bf16[32,8064]{1,0:T(8,128)(2,1)S(1)}, u32[]{:S(2)}, u32[]{:S(2)}) collective-permute-start(bf16[32,8064]{1,0:T(8,128)(2,1)S(1)} %get-tuple-element.159), channel_id=1, source_target_pairs={{0,8},{1,33},{2,10},{3,35},{4,12},{5,37},{6,14},{7,39},{8,0},{9,41... | collective-permute-start | bytes 1548296 | tf_op jit(solution)/shard_map/ppermute | solution.py:51
  315.8 18.9 %collective-permute-start.36 = (bf16[32,8064]{1,0:T(8,128)(2,1)S(1)}, bf16[32,8064]{1,0:T(8,128)(2,1)S(1)}, u32[]{:S(2)}, u32[]{:S(2)}) collective-permute-start(bf16[32,8064]{1,0:T(8,128)(2,1)S(1)} %get-tuple-element.158), channel_id=1, source_target_pairs={{0,12},{1,49},{2,14},{3,51},{4,0},{5,53},{6,2},{7,55},{8,4},{9,57}... | collective-permute-start | bytes 1548296 | tf_op jit(solution)/shard_map/ppermute | solution.py:51
  316.1 16.4 %collective-permute-start.38 = (bf16[64,4608]{1,0:T(8,128)(2,1)S(1)}, bf16[64,4608]{1,0:T(8,128)(2,1)S(1)}, u32[]{:S(2)}, u32[]{:S(2)}) collective-permute-start(bf16[64,4608]{1,0:T(8,128)(2,1)S(1)} %get-tuple-element.154), channel_id=1, source_target_pairs={{0,48},{1,13},{2,50},{3,15},{4,52},{5,1},{6,54},{7,3},{8,56},{9,5}... | collective-permute-start | bytes 1769480 | tf_op jit(solution)/shard_map/ppermute | solution.py:51
  319.0 13.7 %collective-permute-start.37 = (bf16[64,4608]{1,0:T(8,128)(2,1)S(1)}, bf16[64,4608]{1,0:T(8,128)(2,1)S(1)}, u32[]{:S(2)}, u32[]{:S(2)}) collective-permute-start(bf16[64,4608]{1,0:T(8,128)(2,1)S(1)} %get-tuple-element.155), channel_id=1, source_target_pairs={{0,16},{1,5},{2,18},{3,7},{4,20},{5,9},{6,22},{7,11},{8,24},{9,13}... | collective-permute-start | bytes 1769480 | tf_op jit(solution)/shard_map/ppermute | solution.py:51
  336.1 16.2 %collective-permute-start.39 = (bf16[128,4608]{1,0:T(8,128)(2,1)S(1)}, bf16[128,4608]{1,0:T(8,128)(2,1)S(1)}, u32[]{:S(2)}, u32[]{:S(2)}) collective-permute-start(bf16[128,4608]{1,0:T(8,128)(2,1)S(1)} %pad_maximum_fusion.2), channel_id=1, source_target_pairs={{0,16},{1,5},{2,18},{3,7},{4,20},{5,9},{6,22},{7,11},{8,24},{9,13}... | collective-permute-start | bytes 3538952 | tf_op jit(solution)/shard_map/ppermute | solution.py:51
  338.1 16.2 %collective-permute-start.40 = (bf16[128,4608]{1,0:T(8,128)(2,1)S(1)}, bf16[128,4608]{1,0:T(8,128)(2,1)S(1)}, u32[]{:S(2)}, u32[]{:S(2)}) collective-permute-start(bf16[128,4608]{1,0:T(8,128)(2,1)S(1)} %pad_maximum_fusion.3), channel_id=1, source_target_pairs={{0,48},{1,13},{2,50},{3,15},{4,52},{5,1},{6,54},{7,3},{8,56},{9,5}... | collective-permute-start | bytes 3538952 | tf_op jit(solution)/shard_map/ppermute | solution.py:51
  355.1 11.2 %collective-permute-start.42 = (bf16[32,4608]{1,0:T(8,128)(2,1)S(1)}, bf16[32,4608]{1,0:T(8,128)(2,1)S(1)}, u32[]{:S(2)}, u32[]{:S(2)}) collective-permute-start(bf16[32,4608]{1,0:T(8,128)(2,1)S(1)} %get-tuple-element.164), channel_id=1, source_target_pairs={{0,8},{1,33},{2,10},{3,35},{4,12},{5,37},{6,14},{7,39},{8,0},{9,41... | collective-permute-start | bytes 884744 | tf_op jit(solution)/shard_map/ppermute | solution.py:51
  (41 other events, 453.7 us)

commit v2 on v1

--- a/solution.py
+++ b/solution.py
@@ -306,8 +306,6 @@
         dyn = to_absolute(total[...], order[...])
         unit, scale = normal(h[...])
         gain = contract_last(gain_rows(gains).astype(BF), order[...])[1:2]
-        if saves:
-            saves[2][...] = dot((dyn * unit).astype(BF), order[...]).astype(BF)
         grad = dz[...].astype(F32) + normal_back(dyn * gain, unit, scale)
         dh[...] = grad
         da[...] = grad.astype(BF)
@@ -341,7 +339,7 @@
         put(2, at, jnp.concatenate(dvs, 1).astype(BF))
 
 
-def qkv_backward_step(step, steps, dqkv, dh, u, order, gains, proj, du, total, term=None):
+def qkv_backward_step(step, steps, dqkv, dh, u, order, gains, proj, du, total):
     @pl.when(step == 0)
     def _():
         total[...] = jnp.zeros_like(total)
@@ -352,8 +350,6 @@
     def _():
         unit, scale = normal(dot(u[...], order[...]))
         dxn = total[...]
-        if term is not None:
-            term[...] = (dxn * unit).astype(BF)
         back = normal_back(dxn * gain_rows(gains)[0:1], unit, scale)
         du[...] = (dh[...] + to_absolute(back, order[...])).astype(BF)
 
@@ -379,9 +375,9 @@
 
 def mlp_backward_kernel(n, steps, *refs):
     args, (one, two), gains, gate, up, down, rest = parted(refs, 4, 2, n, n, n, n)
-    dg, dv, dh, da, term, total = rest
+    dg, dv, dh, da, total = rest
     weights = (gains, gate, up, down)
-    mlp_backward_step(pl.program_id(0), steps, *args, one[...], two[...], *weights, dh, da, total, (dg, dv, term))
+    mlp_backward_step(pl.program_id(0), steps, *args, one[...], two[...], *weights, dh, da, total, (dg, dv))
 
 
 def heads_backward_kernel(n, micro, *refs):
@@ -433,8 +429,12 @@
 
 
 def qkv_backward_kernel(n, steps, *refs):
-    (dqkv, *args), gains, proj, (du, term, total) = parted(refs, 4, n, n)
-    qkv_backward_step(pl.program_id(0), steps, dqkv[...], *args, gains, proj, du, total, term)
+    (dqkv, *args), gains, proj, (du, total) = parted(refs, 4, n, n)
+    qkv_backward_step(pl.program_id(0), steps, dqkv[...], *args, gains, proj, du, total)
+
+
+def gain_grad(weight, grad, gain):
+    return jnp.sum(weight.astype(F32) * grad, 1) / gain.astype(F32)
 
 
 def columns(pieces, tile, place):
@@ -554,9 +554,9 @@
         + columns(pieces, MLP_TILE, lambda j: j)
         + columns(pieces, MLP_TILE, lambda j: steps + j)
         + columns(pieces, MLP_TILE, lambda j: 2 * steps + j),
-        out_specs=[tiled(tokens, MLP_TILE)] * 2 + [fixed(tokens, width)] * 3,
+        out_specs=[tiled(tokens, MLP_TILE)] * 2 + [fixed(tokens, width)] * 2,
         out_shape=[shape_of(tokens, hidden)] * 2
-        + [shape_of(tokens, width, F32), shape_of(tokens, width), shape_of(tokens, width)],
+        + [shape_of(tokens, width, F32), shape_of(tokens, width)],
         scratch_shapes=[pltpu.VMEM((tokens, width), F32)],
         compiler_params=PARAMS,
         cost_estimate=cost(6 * tokens * hidden * width, 4 * hidden * width),
@@ -588,17 +588,17 @@
         + [whole(a) for a in args]
         + columns(pieces, 128, lambda j: 4 * width // 128)
         + columns(pieces, ATTN_TILE, lambda j: j),
-        out_specs=[fixed(tokens, width), fixed(tokens, width)],
-        out_shape=[shape_of(tokens, width), shape_of(tokens, width)],
+        out_specs=fixed(tokens, width),
+        out_shape=shape_of(tokens, width),
         scratch_shapes=[pltpu.VMEM((tokens, width), F32)],
         compiler_params=PARAMS,
         cost_estimate=cost(2 * tokens * 3 * width * width, 3 * width * width),
     )(dqkv, *args, *pieces, *pieces)
 
 
-def product_kernel(counts, sides, *refs):
+def product_kernel(counts, *refs):
     count = len(counts)
-    lefts, rights, rest = refs[: count + sides], refs[count + sides : 2 * (count + sides)], refs[2 * (count + sides) :]
+    lefts, rights, rest = parted(refs, count, count)
     outs, turned = rest[:-1], rest[-1]
     step = pl.program_id(0)
 
@@ -613,9 +613,6 @@
         @pl.when((step >= begin) & (step < begin + counts[which]))
         def _(which=which):
             value = dot(turned[which], rights[which][...])
-            if sides:
-                beside = sum(dot(turned[k], rights[k][...]) for k in range(count, count + sides))
-                value = jnp.concatenate([value, beside], 1)
             low = 0
             for out in outs:
                 out[...] = value[low : low + out.shape[0]].astype(BF)
@@ -624,29 +621,25 @@
         begin += counts[which]
 
 
-def make_product(lefts, rights, tile, side_lefts=(), side_rights=()):
-    tokens, width = lefts[0].shape
+def make_product(lefts, rights, tile):
+    tokens = lefts[0].shape[0]
     counts = [r.shape[1] // tile for r in rights]
     steps = sum(counts)
     starts = [sum(counts[:k]) for k in range(len(counts))]
-    every = (*lefts, *side_lefts)
-    side = side_rights[0].shape[1] // steps if side_rights else 0
-    out_tile = tile + side
 
     def product(part, sizes):
         span = sum(sizes)
         return pl.pallas_call(
-            functools.partial(product_kernel, counts, len(side_lefts)),
+            functools.partial(product_kernel, counts),
             grid=(steps,),
-            in_specs=[pl.BlockSpec((tokens, span), lambda j: (0, part)) for _ in every]
-            + [tiled(tokens, tile, s, c) for s, c in zip(starts, counts)]
-            + [tiled(tokens, side) for _ in side_rights],
-            out_specs=[tiled(r, out_tile) for r in sizes],
-            out_shape=[shape_of(r, steps * out_tile) for r in sizes],
-            scratch_shapes=[pltpu.VMEM((len(every), span, tokens), BF)],
+            in_specs=[pl.BlockSpec((tokens, span), lambda j: (0, part)) for _ in lefts]
+            + [tiled(tokens, tile, s, c) for s, c in zip(starts, counts)],
+            out_specs=[tiled(r, tile) for r in sizes],
+            out_shape=[shape_of(r, steps * tile) for r in sizes],
+            scratch_shapes=[pltpu.VMEM((len(lefts), span, tokens), BF)],
             compiler_params=PARAMS,
-            cost_estimate=cost(2 * tokens * span * steps * out_tile, span * steps * out_tile),
-        )(*every, *rights, *side_rights)
+            cost_estimate=cost(2 * tokens * span * steps * tile, span * steps * tile),
+        )(*lefts, *rights)
 
     return product
 
@@ -696,7 +689,7 @@
     grad_out = jnp.where(section == 1, last_grad, received)
     half = width // 2
     dzr = dot(grad_out, order).astype(BF)
-    dg, dv, dh, da, term_m = mlp_backward(dzr, grad_out, hid, one, two, pieces_a, pieces_m, order)
+    dg, dv, dh, da = mlp_backward(dzr, grad_out, hid, one, two, pieces_a, pieces_m, order)
     product = make_product((yn, yn, dzr), (dg, dv, mid), MLP_TILE)
     sent_m, yn = tie(product(1, (half,))[0], yn)
     got_m = send(sent_m, "core")
@@ -709,32 +702,29 @@
     far_m, far_m2, dqkv = tie(far_m, far_m2, dqkv)
     *mix_m, dqkv = tie(*ring_mix(after_m, before_m, far_m, far_m2), dqkv)
     near_m = send(mix_m[0], "first", 1), send(mix_m[1], "first", -1)
-    grad_in, term_a = qkv_backward(dqkv, dh, layer_in, order, pieces_a)
-    lane = lax.broadcasted_iota(jnp.int32, (tokens, 4 * GAIN_TILE), 1)
-    picks = ((lane == 0).astype(BF), (lane == 1).astype(BF))
-    product = make_product((xn, attended), (dqkv, da), width, (term_a, term_m), picks)
-    *own_a, sent_a = product(0, (*cut(half), half))
+    grad_in = qkv_backward(dqkv, dh, layer_in, order, pieces_a)
+    dqkv, grad_in = tie(dqkv, grad_in)
+    *own_a, sent_a = make_product((xn, attended), (dqkv, da), width)(0, (*cut(half), half))
     got_a = send(sent_a, "core")
     here_a, after_a, far_a, far_a2, before_a = ring_start(own_a, got_a)
+    far_a, far_a2 = send(far_a.astype(BF), "first", 1), send(far_a2.astype(BF), "first", -1)
     ends_m = direct(ring_close(here_m, *near_m))
-    far_a, far_a2 = send(far_a.astype(BF), "first", 1), send(far_a2.astype(BF), "first", -1)
     mix_a = ring_mix(after_a, before_a, far_a, far_a2)
     *ends_m, mix_a, mix_a2 = tie(*ends_m, *mix_a)
     near_a = send(mix_a, "first", 1), send(mix_a2, "first", -1)
     sum_m = close_z(*ends_m)
     sum_a = close_z(*direct(ring_close(here_a, *near_a)))
-    edge = width + GAIN_TILE
-    grad_proj = jnp.concatenate([sum_a[:, k * edge : k * edge + width] for k in range(3)], 1)
+    grad_proj, grad_out_proj = sum_a[:, :three], sum_a[:, three:]
     grad_up = jnp.concatenate([sum_m[:, :hidden], sum_m[:, padded : padded + hidden]], 1)
     return (
         result.reshape(1, micro, slots, width),
         grad_in.reshape(1, micro, slots, width),
         grad_proj[None],
-        sum_a[:, 3 * edge : 3 * edge + width][None],
+        grad_out_proj[None],
         grad_up[None],
         sum_m[:, 2 * padded : 2 * padded + hidden][None],
-        sum_a[:, width][None],
-        sum_a[:, width + 1][None],
+        gain_grad(attn_proj[0], grad_proj, gain_attn[0])[None],
+        gain_grad(mlp_in[0], grad_up, gain_mlp[0])[None],
     )
 
 

time: 377 us -> 374 us (level)
  no operation moved by 1% of the time
where the time goes in v2:
time: 374 us; the launch traced here: 371 us
  Pallas kernels  145 us (39%)
  waiting for transfers between devices  122 us (33%)
  starting transfers between devices  54.5 us (15%)
  other arithmetic  29.2 us (8%)
  local copies, waits for them, and re-layouts  18.5 us (5%)
    ppermute x44, waiting for transfers between devices, send(): return lax.ppermute(value, 'fsdp', pairs(kind, step))  100 us
    pallas_call x1, Pallas kernels, middle(): pl.pallas_call(functools.partial(middle_kernel, n, common[-1].shape[0]),...  59.7 us
    ppermute x44, starting transfers between devices, send(): return lax.ppermute(value, 'fsdp', pairs(kind, step))  47.7 us
    pallas_call x3, Pallas kernels, product(): pl.pallas_call(functools.partial(product_kernel, counts), grid=(steps,),...  26.4 us
    pallas_call x1, Pallas kernels, mlp_backward(): pl.pallas_call(functools.partial(mlp_backward_kernel, n, steps), grid=(st...  14.8 us
    pallas_call x1, Pallas kernels, attn_forward(): pl.pallas_call(functools.partial(attn_forward_kernel, n, common[-1].shape...  13.3 us
    ppermute x1, waiting for transfers between devices, shards(): received = lax.ppermute(middle_grad, 'section', [(1, 0)])  12.6 us
    pallas_call x1, Pallas kernels, mlp_forward(): pl.pallas_call(functools.partial(mlp_forward_kernel, n, steps), grid=(ste...  12.2 us
  transfers between devices with their start and end apart: 46, of which 29 were waited for; matrix products, arithmetic and copies ran while one was open for 7% of the time, Pallas kernels for 13%

profile of v2, /device:TPU:8, one launch (start us, length us, event | category | flops | bytes accessed | tf_op | source)
XLA Modules:
  0.0 371.3 jit_solution(15966859071611021245)
XLA Ops:
  12.0 2.8 collective-permute-start.1
  31.4 10.0 %collective-permute-done.9 = bf16[32,8064]{1,0:T(8,128)(2,1)S(1)} collective-permute-done((bf16[32,8064]{1,0:T(8,128)(2,1)S(1)}, bf16[32,8064]{1,0:T(8,128)(2,1)S(1)}, u32[]{:S(2)}, u32[]{:S(2)}) %collective-permute-start.9) | collective-permute-done | bytes 516128 | tf_op jit(solution)/shard_map/ppermute | solution.py:51
  45.2 4.8 %collective-permute-done.5.refs_7_.refs_17_.refs_27_.refs_8_.refs_18_.refs_28_.refs_9_.refs_5_.refs_15_ = bf16[128,4224]{1,0:T(8,128)(2,1)S(1)} collective-permute-done((bf16[128,4224]{1,0:T(8,128)(2,1)}, bf16[128,4224]{1,0:T(8,128)(2,1)S(1)}, u32[]{:S(2)}, u32[]{:S(2)}) %collective-permute-start.5) | collective-permute-done | bytes 1081376 | tf_op jit(solution)/shard_map/ppermute | solution.py:51
  53.3 6.2 %collective-permute-done.6.refs_8_.refs_18_.refs_28_.refs_9_.refs_19_.refs_29_.refs_10_.refs_6_.refs_16_ = bf16[64,4224]{1,0:T(8,128)(2,1)} collective-permute-done((bf16[64,4224]{1,0:T(8,128)(2,1)S(1)}, bf16[64,4224]{1,0:T(8,128)(2,1)}, u32[]{:S(2)}, u32[]{:S(2)}) %collective-permute-start.6) | collective-permute-done | bytes 540704 | tf_op jit(solution)/shard_map/ppermute | solution.py:51
  59.5 3.0 collective-permute-done.8.refs_9_.refs_19_.refs_29_.refs_10_.refs_20_.refs_30_.refs_11_.refs_7_.refs_17_
  62.5 3.2 collective-permute-start.12
  73.5 13.3 %shard_map.152 = (f32[192,1024]{1,0:T(8,128)}, bf16[192,1024]{1,0:T(8,128)(2,1)}) custom-call(bf16[192,1024]{1,0:T(8,128)(2,1)} %bitcast.47, bf16[1024,1024]{1,0:T(8,128)(2,1)} %fusion.refs_1_.refs_2_.refs_3_, f32[192,128]{1,0:T(8,128)} %copy.47.refs_2_.refs_3_, f32[192,128]{1,0:T(8,128)} %copy.48.refs_3_.refs_4_, ...), custom_call_target="tpu_custom_call" | custom-call | flops 37748736 | bytes 163840 | tf_op jit(solution)/shard_map/pallas_call | solution.py:470
  95.8 10.7 %collective-permute-done.19.refs_5_.refs_15_.refs_25_.refs_39_.refs_49_.refs_59_.refs_18_.refs_28_.refs_38_ = bf16[64,8064]{1,0:T(8,128)(2,1)S(1)} collective-permute-done((bf16[64,8064]{1,0:T(8,128)(2,1)S(1)}, bf16[64,8064]{1,0:T(8,128)(2,1)S(1)}, u32[]{:S(2)}, u32[]{:S(2)}) %collective-permute-start.19) | collective-permute-done | bytes 1032224 | tf_op jit(solution)/shard_map/ppermute | solution.py:51
  113.4 12.2 %shard_map.153 = bf16[192,1024]{1,0:T(8,128)(2,1)} custom-call(bf16[192,1024]{1,0:T(8,128)(2,1)} %get-tuple-element.98.refs_0_, f32[192,1024]{1,0:T(8,128)} %get-tuple-element.99.refs_1_, bf16[1024,1024]{1,0:T(8,128)(2,1)} %fusion.refs_1_.refs_2_.refs_3_, ...), custom_call_target="tpu_custom_call" | custom-call | flops 49545216 | bytes 344064 | tf_op jit(solution)/shard_map/pallas_call | solution.py:490
  125.6 5.5 %collective-permute-start.26 = (bf16[192,1024]{1,0:T(8,128)(2,1)}, bf16[192,1024]{1,0:T(8,128)(2,1)S(1)}, u32[]{:S(2)}, u32[]{:S(2)}) collective-permute-start(bf16[192,1024]{1,0:T(8,128)(2,1)} %shard_map.153), channel_id=1, source_target_pairs={{0,64},{1,65},{2,66},{3,67},{4,68},{5,69},{6,70},{7,71},{8,72},{9,... | collective-permute-start | bytes 1179656 | tf_op jit(solution)/shard_map/ppermute | solution.py:682
  131.1 9.0 %collective-permute-done.26 = bf16[192,1024]{1,0:T(8,128)(2,1)S(1)} collective-permute-done((bf16[192,1024]{1,0:T(8,128)(2,1)}, bf16[192,1024]{1,0:T(8,128)(2,1)S(1)}, u32[]{:S(2)}, u32[]{:S(2)}) %collective-permute-start.26) | collective-permute-done | bytes 393248 | tf_op jit(solution)/shard_map/ppermute | solution.py:682
  140.9 59.7 %shard_map.154 = (bf16[192,1024]{1,0:T(8,128)(2,1)}, bf16[3,192,1024]{2,1,0:T(8,128)(2,1)}, f32[192,128]{1,0:T(8,128)}, bf16[192,1024]{1,0:T(8,128)(2,1)}, f32[1...) custom-call(bf16[192,1024]{1,0:T(8,128)(2,1)} %broadcast_select_fusi, ...), custom_call_target="tpu_custom_call" | custom-call | flops 136839168 | bytes 1032192 | tf_op jit(solution)/shard_map/pallas_call | solution.py:519
  201.9 12.6 %collective-permute-done.27 = bf16[192,1024]{1,0:T(8,128)(2,1)S(1)} collective-permute-done((bf16[192,1024]{1,0:T(8,128)(2,1)}, bf16[192,1024]{1,0:T(8,128)(2,1)S(1)}, u32[]{:S(2)}, u32[]{:S(2)}) %collective-permute-start.27) | collective-permute-done | bytes 393248 | tf_op jit(solution)/shard_map/ppermute | solution.py:688
  216.0 14.8 %shard_map.155 = (bf16[192,2688]{1,0:T(8,128)(2,1)}, bf16[192,2688]{1,0:T(8,128)(2,1)}, f32[192,1024]{1,0:T(8,128)}, bf16[192,1024]{1,0:T(8,128)(2,1)}) custom-call(bf16[192,1024]{1,0:T(8,128)(2,1)} %convolution_convert_fusion.refs_0_.refs_2_, bf16[192,1024]{1,0:T(8,128)(2,1)} %copy-done.12, f32[192,1024]{1,0:T(8,128)} %get-tuple-element.105.refs_2_, ...), custom_call_target="tpu_custom_call" | custom-call | flops 49545216 | bytes 344064 | tf_op jit(solution)/shard_map/pallas_call | solution.py:548
  230.9 9.7 %shard_map.156 = bf16[512,8064]{1,0:T(8,128)(2,1)} custom-call(bf16[192,1024]{1,0:T(8,128)(2,1)} %get-tuple-element.111.refs_0_.refs_1_, bf16[192,1024]{1,0:T(8,128)(2,1)} %get-tuple-element.111.refs_0_.refs_1_, bf16[192,1024]{1,0:T(8,128)(2,1)} %convolution_convert_fusion.refs_0_.refs_2_, bf16[192,2688]{1,0:T(8,128)(2,1)} %get-tuple-element.108.refs_3_, ...), custom_call_target="tpu_custom_call" | custom-call | flops 24772608 | bytes 129024 | tf_op jit(solution)/shard_map/pallas_call | solution.py:632
  240.6 9.8 %shard_map.157 = (bf16[128,8064]{1,0:T(8,128)(2,1)}, bf16[128,8064]{1,0:T(8,128)(2,1)}, bf16[64,8064]{1,0:T(8,128)(2,1)}, bf16[64,8064]{1,0:T(8,128)(2,1)}, bf16[128,8064]{1,0:T(8,128)(2,1)}) custom-call(bf16[192,1024]{1,0:T(8,128)(2,1)} %get-tuple-element.111.refs_0_.refs_1_, bf16[192,1024]{1,0:T(8,128)(2,1)} %get-tuple-element.111.refs_0_.refs_1_, ...), custom_call_target="tpu_custom_call" | custom-call | flops 24772608 | bytes 129024 | tf_op jit(solution)/shard_map/pallas_call | solution.py:632
  250.4 3.5 collective-permute-done.28
  253.9 4.1 %add_convert_fusion.2 = (bf16[64,8064]{1,0:T(8,128)(2,1)}, bf16[64,8064]{1,0:T(8,128)(2,1)}) fusion(bf16[64,8064]{1,0:T(8,128)(2,1)} %get-tuple-element.117, bf16[512,8064]{1,0:T(8,128)(2,1)} %collective-permute-done.28, bf16[64,8064]{1,0:T(8,128)(2,1)} %get-tuple-element.116), kind=kLoop, calls=%fused_computation.16 | loop fusion | flops 4128768 | bytes 6193152 | tf_op jit(solution)/shard_map/convert_element_type | solution.py:700
  260.1 3.1 convert_add_fusion
  265.4 8.8 %shard_map.158.refs_0_.refs_2_ = bf16[192,3072]{1,0:T(8,128)(2,1)} custom-call(bf16[192,1024]{1,0:T(8,128)(2,1)} %get-tuple-element.118.refs_0_.refs_3_, bf16[1024,1024]{1,0:T(8,128)(2,1)} %fusion.refs_1_.refs_2_.refs_3_, f32[192,128]{1,0:T(8,128)} %copy.47.refs_2_.refs_3_, f32[192,128]{1,0:T(8,128)} %copy.48.refs_3_.refs_4_, ...), custom_call_target="tpu_custom_call" | custom-call | flops 6291456 | bytes 32768 | tf_op jit(solution)/shard_map/pallas_call | solution.py:569
  281.3 9.4 %shard_map.159 = bf16[192,1024]{1,0:T(8,128)(2,1)} custom-call(bf16[192,3072]{1,0:T(8,128)(2,1)} %shard_map.158.refs_0_.refs_2_, f32[192,1024]{1,0:T(8,128)} %get-tuple-element.126.refs_1_, bf16[192,1024]{1,0:T(8,128)(2,1)} %broadcast_select_fusion.1.refs_0_.refs_2_, bf16[1024,1024]{1,0:T(8,128)(2,1)} %fusion.refs_1_.refs_2_.refs_3_, ...), custom_call_target="tpu_custom_call" | custom-call | flops 18874368 | bytes 98304 | tf_op jit(solution)/shard_map/pallas_call | solution.py:584
  290.7 6.9 %shard_map.160 = (bf16[128,4096]{1,0:T(8,128)(2,1)}, bf16[128,4096]{1,0:T(8,128)(2,1)}, bf16[64,4096]{1,0:T(8,128)(2,1)}, bf16[64,4096]{1,0:T(8,128)(2,1)}, bf16...) custom-call(bf16[192,1024]{1,0:T(8,128)(2,1)} %get-tuple-element.128.refs_0_, ...), custom_call_target="tpu_custom_call" | custom-call | flops 25165824 | bytes 131072 | tf_op jit(solution)/shard_map/pallas_call | solution.py:632
  297.6 3.0 collective-permute-start.31
  300.6 4.5 %collective-permute-done.32 = bf16[128,8064]{1,0:T(8,128)(2,1)S(1)} collective-permute-done((bf16[128,8064]{1,0:T(8,128)(2,1)}, bf16[128,8064]{1,0:T(8,128)(2,1)S(1)}, u32[]{:S(2)}, u32[]{:S(2)}) %collective-permute-start.32) | collective-permute-done | bytes 2064416 | tf_op jit(solution)/shard_map/ppermute | solution.py:51
  306.3 2.6 add_convert_fusion
  310.8 4.5 %collective-permute-start.35 = (bf16[32,8064]{1,0:T(8,128)(2,1)S(1)}, bf16[32,8064]{1,0:T(8,128)(2,1)S(1)}, u32[]{:S(2)}, u32[]{:S(2)}) collective-permute-start(bf16[32,8064]{1,0:T(8,128)(2,1)S(1)} %get-tuple-element.155), channel_id=1, source_target_pairs={{0,8},{1,33},{2,10},{3,35},{4,12},{5,37},{6,14},{7,39},{8,0},{9,41... | collective-permute-start | bytes 1548296 | tf_op jit(solution)/shard_map/ppermute | solution.py:51
  318.6 12.8 %collective-permute-done.38 = bf16[64,4096]{1,0:T(8,128)(2,1)S(1)} collective-permute-done((bf16[64,4096]{1,0:T(8,128)(2,1)S(1)}, bf16[64,4096]{1,0:T(8,128)(2,1)S(1)}, u32[]{:S(2)}, u32[]{:S(2)}) %collective-permute-start.38) | collective-permute-done | bytes 524320 | tf_op jit(solution)/shard_map/ppermute | solution.py:51
  336.9 4.7 %collective-permute-done.45 = bf16[16,8064]{1,0:T(8,128)(2,1)S(1)} collective-permute-done((bf16[16,8064]{1,0:T(8,128)(2,1)S(1)}, bf16[16,8064]{1,0:T(8,128)(2,1)S(1)}, u32[]{:S(2)}, u32[]{:S(2)}) %collective-permute-start.45) | collective-permute-done | bytes 258080 | tf_op jit(solution)/shard_map/ppermute | solution.py:51
  341.7 8.0 %collective-permute-done.39 = bf16[128,4096]{1,0:T(8,128)(2,1)S(1)} collective-permute-done((bf16[128,4096]{1,0:T(8,128)(2,1)S(1)}, bf16[128,4096]{1,0:T(8,128)(2,1)S(1)}, u32[]{:S(2)}, u32[]{:S(2)}) %collective-permute-start.39) | collective-permute-done | bytes 1048608 | tf_op jit(solution)/shard_map/ppermute | solution.py:51
  352.5 4.0 %collective-permute-start.42 = (bf16[32,4096]{1,0:T(8,128)(2,1)S(1)}, bf16[32,4096]{1,0:T(8,128)(2,1)S(1)}, u32[]{:S(2)}, u32[]{:S(2)}) collective-permute-start(bf16[32,4096]{1,0:T(8,128)(2,1)S(1)} %get-tuple-element.160), channel_id=1, source_target_pairs={{0,8},{1,33},{2,10},{3,35},{4,12},{5,37},{6,14},{7,39},{8,0},{9,41... | collective-permute-start | bytes 786440 | tf_op jit(solution)/shard_map/ppermute | solution.py:51
  360.1 3.6 collective-permute-done.42
  365.6 3.4 collective-permute-done.44
  (214 shorter events, 95.6 us)
Async XLA Ops:
  15.6 10.1 %collective-permute-start.3 = (bf16[32,4224]{1,0:T(8,128)(2,1)S(1)}, bf16[32,4224]{1,0:T(8,128)(2,1)S(1)}, u32[]{:S(2)}, u32[]{:S(2)}) collective-permute-start(bf16[32,4224]{1,0:T(8,128)(2,1)S(1)} %pad_maximum_fusion.5), channel_id=1, source_target_pairs={{0,4},{1,17},{2,6},{3,19},{4,8},{5,21},{6,10},{7,23},{8,12},{9,25}... | collective-permute-start | bytes 811016 | tf_op jit(solution)/shard_map/ppermute | solution.py:51
  16.5 9.9 %collective-permute-start.4 = (bf16[16,8064]{1,0:T(8,128)(2,1)S(1)}, bf16[16,8064]{1,0:T(8,128)(2,1)S(1)}, u32[]{:S(2)}, u32[]{:S(2)}) collective-permute-start(bf16[16,8064]{1,0:T(8,128)(2,1)S(1)} %concatenate.47), channel_id=1, source_target_pairs={{0,2},{1,3},{2,0},{3,1},{4,6},{5,7},{6,4},{7,5},{8,10},{9,11},{10,... | collective-permute-start | bytes 774152 | tf_op jit(solution)/shard_map/ppermute | solution.py:51
  27.2 14.3 %collective-permute-start.9 = (bf16[32,8064]{1,0:T(8,128)(2,1)S(1)}, bf16[32,8064]{1,0:T(8,128)(2,1)S(1)}, u32[]{:S(2)}, u32[]{:S(2)}) collective-permute-start(bf16[32,8064]{1,0:T(8,128)(2,1)S(1)} %get-tuple-element.168), channel_id=1, source_target_pairs={{0,12},{1,49},{2,14},{3,51},{4,0},{5,53},{6,2},{7,55},{8,4},{9,57}... | collective-permute-start | bytes 1548296 | tf_op jit(solution)/shard_map/ppermute | solution.py:51
  28.3 16.0 %collective-permute-start.10 = (bf16[32,8064]{1,0:T(8,128)(2,1)S(1)}, bf16[32,8064]{1,0:T(8,128)(2,1)S(1)}, u32[]{:S(2)}, u32[]{:S(2)}) collective-permute-start(bf16[32,8064]{1,0:T(8,128)(2,1)S(1)} %get-tuple-element.168), channel_id=1, source_target_pairs={{0,8},{1,33},{2,10},{3,35},{4,12},{5,37},{6,14},{7,39},{8,0},{9,41... | collective-permute-start | bytes 1548296 | tf_op jit(solution)/shard_map/ppermute | solution.py:51
  28.5 23.9 %collective-permute-start.11 = (bf16[32,8064]{1,0:T(8,128)(2,1)S(1)}, bf16[32,8064]{1,0:T(8,128)(2,1)S(1)}, u32[]{:S(2)}, u32[]{:S(2)}) collective-permute-start(bf16[32,8064]{1,0:T(8,128)(2,1)S(1)} %get-tuple-element.168), channel_id=1, source_target_pairs={{0,4},{1,17},{2,6},{3,19},{4,8},{5,21},{6,10},{7,23},{8,12},{9,25}... | collective-permute-start | bytes 1548296 | tf_op jit(solution)/shard_map/ppermute | solution.py:51
  29.4 20.6 %collective-permute-start.5 = (bf16[128,4224]{1,0:T(8,128)(2,1)}, bf16[128,4224]{1,0:T(8,128)(2,1)S(1)}, u32[]{:S(2)}, u32[]{:S(2)}) collective-permute-start(bf16[128,4224]{1,0:T(8,128)(2,1)} %constant_dynamic-update-slice_fusion.refs_6_.refs_16_.refs_26_.refs_7_.refs_17_.refs_27_.refs_8_.refs_4_.refs_14_), channel_id=1, source_target_pairs={{0,48},{1,13},{2,50},{3,15},{4,52},{5,1},{6,54},{7,3},{8,56},{9,5}... | collective-permute-start | bytes 3244040 | tf_op jit(solution)/shard_map/ppermute | solution.py:51
  29.8 21.7 %collective-permute-start.7 = (bf16[128,4224]{1,0:T(8,128)(2,1)}, bf16[128,4224]{1,0:T(8,128)(2,1)S(1)}, u32[]{:S(2)}, u32[]{:S(2)}) collective-permute-start(bf16[128,4224]{1,0:T(8,128)(2,1)} %constant_dynamic-update-slice_fusion.refs_6_.refs_16_.refs_26_.refs_7_.refs_17_.refs_27_.refs_8_.refs_4_.refs_14_), channel_id=1, source_target_pairs={{0,16},{1,5},{2,18},{3,7},{4,20},{5,9},{6,22},{7,11},{8,24},{9,13}... | collective-permute-start | bytes 3244040 | tf_op jit(solution)/shard_map/ppermute | solution.py:51
  41.5 25.9 %collective-permute-start.14 = (bf16[128,4224]{1,0:T(8,128)(2,1)}, bf16[128,4224]{1,0:T(8,128)(2,1)}, u32[]{:S(2)}, u32[]{:S(2)}) collective-permute-start(bf16[128,4224]{1,0:T(8,128)(2,1)} %constant_dynamic-update-slice_fusion.refs_6_.refs_16_.refs_26_.refs_7_.refs_17_.refs_27_.refs_8_.refs_4_.refs_14_), channel_id=1, source_target_pairs={{0,1},{1,0},{2,3},{3,2},{4,5},{5,4},{6,7},{7,6},{8,9},{9,8},{10,11... | collective-permute-start | bytes 3244040 | tf_op jit(solution)/shard_map/ppermute | solution.py:51
  51.6 10.9 %collective-permute-start.8 = (bf16[64,4224]{1,0:T(8,128)(2,1)S(1)}, bf16[64,4224]{1,0:T(8,128)(2,1)}, u32[]{:S(2)}, u32[]{:S(2)}) collective-permute-start(bf16[64,4224]{1,0:T(8,128)(2,1)S(1)} %slice.198), channel_id=1, source_target_pairs={{0,16},{1,5},{2,18},{3,7},{4,20},{5,9},{6,22},{7,11},{8,24},{9,13}... | collective-permute-start | bytes 1622024 | tf_op jit(solution)/shard_map/ppermute | solution.py:51
  62.5 26.7 %collective-permute-start.12 = (bf16[128,8064]{1,0:T(8,128)(2,1)}, bf16[128,8064]{1,0:T(8,128)(2,1)S(1)}, u32[]{:S(2)}, u32[]{:S(2)}) collective-permute-start(bf16[128,8064]{1,0:T(8,128)(2,1)} %constant_dynamic-update-slice_fusion.7.refs_3_.refs_13_.refs_23_.refs_37_.refs_47_.refs_57_.refs_16_.refs_26_.refs_36_), channel_id=1, source_target_pairs={{0,48},{1,13},{2,50},{3,15},{4,52},{5,1},{6,54},{7,3},{8,56},{9,5}... | collective-permute-start | bytes 6193160 | tf_op jit(solution)/shard_map/ppermute | solution.py:51
  65.8 26.0 %collective-permute-start.13 = (bf16[128,8064]{1,0:T(8,128)(2,1)}, bf16[128,8064]{1,0:T(8,128)(2,1)}, u32[]{:S(2)}, u32[]{:S(2)}) collective-permute-start(bf16[128,8064]{1,0:T(8,128)(2,1)} %constant_dynamic-update-slice_fusion.7.refs_3_.refs_13_.refs_23_.refs_37_.refs_47_.refs_57_.refs_16_.refs_26_.refs_36_), channel_id=1, source_target_pairs={{0,16},{1,5},{2,18},{3,7},{4,20},{5,9},{6,22},{7,11},{8,24},{9,13}... | collective-permute-start | bytes 6193160 | tf_op jit(solution)/shard_map/ppermute | solution.py:51
  73.0 36.1 %collective-permute-start.21 = (bf16[128,8064]{1,0:T(8,128)(2,1)}, bf16[128,8064]{1,0:T(8,128)(2,1)S(1)}, u32[]{:S(2)}, u32[]{:S(2)}) collective-permute-start(bf16[128,8064]{1,0:T(8,128)(2,1)} %constant_dynamic-update-slice_fusion.7.refs_3_.refs_13_.refs_23_.refs_37_.refs_47_.refs_57_.refs_16_.refs_26_.refs_36_), channel_id=1, source_target_pairs={{0,1},{1,0},{2,3},{3,2},{4,5},{5,4},{6,7},{7,6},{8,9},{9,8},{10,11... | collective-permute-start | bytes 6193160 | tf_op jit(solution)/shard_map/ppermute | solution.py:51
  91.8 14.7 %collective-permute-start.19 = (bf16[64,8064]{1,0:T(8,128)(2,1)S(1)}, bf16[64,8064]{1,0:T(8,128)(2,1)S(1)}, u32[]{:S(2)}, u32[]{:S(2)}) collective-permute-start(bf16[64,8064]{1,0:T(8,128)(2,1)S(1)} %slice.160), channel_id=1, source_target_pairs={{0,48},{1,13},{2,50},{3,15},{4,52},{5,1},{6,54},{7,3},{8,56},{9,5}... | collective-permute-start | bytes 3096584 | tf_op jit(solution)/shard_map/ppermute | solution.py:51
  94.4 14.7 %collective-permute-start.20 = (bf16[64,8064]{1,0:T(8,128)(2,1)S(1)}, bf16[64,8064]{1,0:T(8,128)(2,1)S(1)}, u32[]{:S(2)}, u32[]{:S(2)}) collective-permute-start(bf16[64,8064]{1,0:T(8,128)(2,1)S(1)} %slice.161), channel_id=1, source_target_pairs={{0,16},{1,5},{2,18},{3,7},{4,20},{5,9},{6,22},{7,11},{8,24},{9,13}... | collective-permute-start | bytes 3096584 | tf_op jit(solution)/shard_map/ppermute | solution.py:51
  95.3 16.5 %collective-permute-start.22 = (bf16[128,8064]{1,0:T(8,128)(2,1)S(1)}, bf16[128,8064]{1,0:T(8,128)(2,1)S(1)}, u32[]{:S(2)}, u32[]{:S(2)}) collective-permute-start(bf16[128,8064]{1,0:T(8,128)(2,1)S(1)} %collective-permute-done.12.refs_4_.refs_14_.refs_24_.refs_38_.refs_48_.refs_58_.refs_17_.refs_27_.refs_37_), channel_id=1, source_target_pairs={{0,1},{1,0},{2,3},{3,2},{4,5},{5,4},{6,7},{7,6},{8,9},{9,8},{10,11... | collective-permute-start | bytes 6193160 | tf_op jit(solution)/shard_map/ppermute | solution.py:51
  95.3 16.5 %collective-permute-start.25 = (bf16[128,8064]{1,0:T(8,128)(2,1)}, bf16[128,8064]{1,0:T(8,128)(2,1)}, u32[]{:S(2)}, u32[]{:S(2)}) collective-permute-start(bf16[128,8064]{1,0:T(8,128)(2,1)} %collective-permute-done.13.refs_7_.refs_17_.refs_27_.refs_41_.refs_51_.refs_61_.refs_20_.refs_30_.refs_40_), channel_id=1, source_target_pairs={{0,1},{1,0},{2,3},{3,2},{4,5},{5,4},{6,7},{7,6},{8,9},{9,8},{10,11... | collective-permute-start | bytes 6193160 | tf_op jit(solution)/shard_map/ppermute | solution.py:51
  125.6 14.5 %collective-permute-start.26 = (bf16[192,1024]{1,0:T(8,128)(2,1)}, bf16[192,1024]{1,0:T(8,128)(2,1)S(1)}, u32[]{:S(2)}, u32[]{:S(2)}) collective-permute-start(bf16[192,1024]{1,0:T(8,128)(2,1)} %shard_map.153), channel_id=1, source_target_pairs={{0,64},{1,65},{2,66},{3,67},{4,68},{5,69},{6,70},{7,71},{8,72},{9,... | collective-permute-start | bytes 1179656 | tf_op jit(solution)/shard_map/ppermute | solution.py:682
  200.6 13.9 %collective-permute-start.27 = (bf16[192,1024]{1,0:T(8,128)(2,1)}, bf16[192,1024]{1,0:T(8,128)(2,1)S(1)}, u32[]{:S(2)}, u32[]{:S(2)}) collective-permute-start(bf16[192,1024]{1,0:T(8,128)(2,1)} %get-tuple-element.104), channel_id=1, source_target_pairs={{64,0},{65,1},{66,2},{67,3},{68,4},{69,5},{70,6},{71,7},{72,8},{73... | collective-permute-start | bytes 1179656 | tf_op jit(solution)/shard_map/ppermute | solution.py:688
  240.6 13.3 %collective-permute-start.28 = (bf16[512,8064]{1,0:T(8,128)(2,1)}, bf16[512,8064]{1,0:T(8,128)(2,1)}, u32[]{:S(2)}, u32[]{:S(2)}) collective-permute-start(bf16[512,8064]{1,0:T(8,128)(2,1)} %shard_map.156), channel_id=1, source_target_pairs={{0,1},{1,0},{2,3},{3,2},{4,5},{5,4},{6,7},{7,6},{8,9},{9,8},{10,11... | collective-permute-start | bytes 24772616 | tf_op jit(solution)/shard_map/ppermute | solution.py:51
  257.9 16.2 %collective-permute-start.29 = (bf16[64,8064]{1,0:T(8,128)(2,1)}, bf16[64,8064]{1,0:T(8,128)(2,1)}, u32[]{:S(2)}, u32[]{:S(2)}) collective-permute-start(bf16[64,8064]{1,0:T(8,128)(2,1)} %get-tuple-element.149), channel_id=1, source_target_pairs={{0,16},{1,5},{2,18},{3,7},{4,20},{5,9},{6,22},{7,11},{8,24},{9,13}... | collective-permute-start | bytes 3096584 | tf_op jit(solution)/shard_map/ppermute | solution.py:51
  258.8 15.4 %collective-permute-start.30 = (bf16[64,8064]{1,0:T(8,128)(2,1)}, bf16[64,8064]{1,0:T(8,128)(2,1)}, u32[]{:S(2)}, u32[]{:S(2)}) collective-permute-start(bf16[64,8064]{1,0:T(8,128)(2,1)} %get-tuple-element.148), channel_id=1, source_target_pairs={{0,48},{1,13},{2,50},{3,15},{4,52},{5,1},{6,54},{7,3},{8,56},{9,5}... | collective-permute-start | bytes 3096584 | tf_op jit(solution)/shard_map/ppermute | solution.py:51
  278.8 26.3 %collective-permute-start.32 = (bf16[128,8064]{1,0:T(8,128)(2,1)}, bf16[128,8064]{1,0:T(8,128)(2,1)S(1)}, u32[]{:S(2)}, u32[]{:S(2)}) collective-permute-start(bf16[128,8064]{1,0:T(8,128)(2,1)} %pad_maximum_fusion), channel_id=1, source_target_pairs={{0,16},{1,5},{2,18},{3,7},{4,20},{5,9},{6,22},{7,11},{8,24},{9,13}... | collective-permute-start | bytes 6193160 | tf_op jit(solution)/shard_map/ppermute | solution.py:51
  279.6 26.7 %collective-permute-start.33 = (bf16[128,8064]{1,0:T(8,128)(2,1)S(1)}, bf16[128,8064]{1,0:T(8,128)(2,1)S(1)}, u32[]{:S(2)}, u32[]{:S(2)}) collective-permute-start(bf16[128,8064]{1,0:T(8,128)(2,1)S(1)} %pad_maximum_fusion.1), channel_id=1, source_target_pairs={{0,48},{1,13},{2,50},{3,15},{4,52},{5,1},{6,54},{7,3},{8,56},{9,5}... | collective-permute-start | bytes 6193160 | tf_op jit(solution)/shard_map/ppermute | solution.py:51
  297.6 17.7 %collective-permute-start.31 = (bf16[512,4096]{1,0:T(8,128)(2,1)}, bf16[512,4096]{1,0:T(8,128)(2,1)S(1)}, u32[]{:S(2)}, u32[]{:S(2)}) collective-permute-start(bf16[512,4096]{1,0:T(8,128)(2,1)} %get-tuple-element.132), channel_id=1, source_target_pairs={{0,1},{1,0},{2,3},{3,2},{4,5},{5,4},{6,7},{7,6},{8,9},{9,8},{10,11... | collective-permute-start | bytes 12582920 | tf_op jit(solution)/shard_map/ppermute | solution.py:51
  309.1 22.7 %collective-permute-start.34 = (bf16[32,8064]{1,0:T(8,128)(2,1)S(1)}, bf16[32,8064]{1,0:T(8,128)(2,1)S(1)}, u32[]{:S(2)}, u32[]{:S(2)}) collective-permute-start(bf16[32,8064]{1,0:T(8,128)(2,1)S(1)} %get-tuple-element.156), channel_id=1, source_target_pairs={{0,4},{1,17},{2,6},{3,19},{4,8},{5,21},{6,10},{7,23},{8,12},{9,25}... | collective-permute-start | bytes 1548296 | tf_op jit(solution)/shard_map/ppermute | solution.py:51
  310.8 22.7 %collective-permute-start.35 = (bf16[32,8064]{1,0:T(8,128)(2,1)S(1)}, bf16[32,8064]{1,0:T(8,128)(2,1)S(1)}, u32[]{:S(2)}, u32[]{:S(2)}) collective-permute-start(bf16[32,8064]{1,0:T(8,128)(2,1)S(1)} %get-tuple-element.155), channel_id=1, source_target_pairs={{0,8},{1,33},{2,10},{3,35},{4,12},{5,37},{6,14},{7,39},{8,0},{9,41... | collective-permute-start | bytes 1548296 | tf_op jit(solution)/shard_map/ppermute | solution.py:51
  315.3 18.2 %collective-permute-start.36 = (bf16[32,8064]{1,0:T(8,128)(2,1)S(1)}, bf16[32,8064]{1,0:T(8,128)(2,1)S(1)}, u32[]{:S(2)}, u32[]{:S(2)}) collective-permute-start(bf16[32,8064]{1,0:T(8,128)(2,1)S(1)} %get-tuple-element.154), channel_id=1, source_target_pairs={{0,12},{1,49},{2,14},{3,51},{4,0},{5,53},{6,2},{7,55},{8,4},{9,57}... | collective-permute-start | bytes 1548296 | tf_op jit(solution)/shard_map/ppermute | solution.py:51
  315.6 15.8 %collective-permute-start.38 = (bf16[64,4096]{1,0:T(8,128)(2,1)S(1)}, bf16[64,4096]{1,0:T(8,128)(2,1)S(1)}, u32[]{:S(2)}, u32[]{:S(2)}) collective-permute-start(bf16[64,4096]{1,0:T(8,128)(2,1)S(1)} %get-tuple-element.150), channel_id=1, source_target_pairs={{0,48},{1,13},{2,50},{3,15},{4,52},{5,1},{6,54},{7,3},{8,56},{9,5}... | collective-permute-start | bytes 1572872 | tf_op jit(solution)/shard_map/ppermute | solution.py:51
  318.4 13.0 %collective-permute-start.37 = (bf16[64,4096]{1,0:T(8,128)(2,1)S(1)}, bf16[64,4096]{1,0:T(8,128)(2,1)S(1)}, u32[]{:S(2)}, u32[]{:S(2)}) collective-permute-start(bf16[64,4096]{1,0:T(8,128)(2,1)S(1)} %get-tuple-element.151), channel_id=1, source_target_pairs={{0,16},{1,5},{2,18},{3,7},{4,20},{5,9},{6,22},{7,11},{8,24},{9,13}... | collective-permute-start | bytes 1572872 | tf_op jit(solution)/shard_map/ppermute | solution.py:51
  334.9 14.8 %collective-permute-start.39 = (bf16[128,4096]{1,0:T(8,128)(2,1)S(1)}, bf16[128,4096]{1,0:T(8,128)(2,1)S(1)}, u32[]{:S(2)}, u32[]{:S(2)}) collective-permute-start(bf16[128,4096]{1,0:T(8,128)(2,1)S(1)} %pad_maximum_fusion.2), channel_id=1, source_target_pairs={{0,16},{1,5},{2,18},{3,7},{4,20},{5,9},{6,22},{7,11},{8,24},{9,13}... | collective-permute-start | bytes 3145736 | tf_op jit(solution)/shard_map/ppermute | solution.py:51
  336.9 14.8 %collective-permute-start.40 = (bf16[128,4096]{1,0:T(8,128)(2,1)S(1)}, bf16[128,4096]{1,0:T(8,128)(2,1)S(1)}, u32[]{:S(2)}, u32[]{:S(2)}) collective-permute-start(bf16[128,4096]{1,0:T(8,128)(2,1)S(1)} %pad_maximum_fusion.3), channel_id=1, source_target_pairs={{0,48},{1,13},{2,50},{3,15},{4,52},{5,1},{6,54},{7,3},{8,56},{9,5}... | collective-permute-start | bytes 3145736 | tf_op jit(solution)/shard_map/ppermute | solution.py:51
  352.5 11.1 %collective-permute-start.42 = (bf16[32,4096]{1,0:T(8,128)(2,1)S(1)}, bf16[32,4096]{1,0:T(8,128)(2,1)S(1)}, u32[]{:S(2)}, u32[]{:S(2)}) collective-permute-start(bf16[32,4096]{1,0:T(8,128)(2,1)S(1)} %get-tuple-element.160), channel_id=1, source_target_pairs={{0,8},{1,33},{2,10},{3,35},{4,12},{5,37},{6,14},{7,39},{8,0},{9,41... | collective-permute-start | bytes 786440 | tf_op jit(solution)/shard_map/ppermute | solution.py:51
  (45 other events, 498.9 us)
